TPU v7x, 32 devices: a whole 2x2x4 slice. The times are simulated.
32 devices in a mesh: dp: 4 (over y, core), blk: 8 (over z, x).
Axes of the slice: x: 2, y: 2, z: 4, core: 2. Of those that a mesh axis runs over, the one named last changes fastest.
Arguments:
- dec_in: bfloat16 [4, 4096, 768], P('dp', 'blk'), may hold values from -6 to 6
- encodings: bfloat16 [4, 1024, 768], P('dp', 'blk'), may hold values from -6 to 6
- enc_question: int32 [4, 1024], P('dp', 'blk'), may hold values from 0 to 3, as said below
- enc_valid: int32 [4, 1024], P('dp', 'blk'), may hold values from 0 to 1, as said below
- tgt_question: int32 [4, 128], P('dp', 'blk'), may hold values from 0 to 3, as said below
- gain_self: float32 [768], replicated, may hold values from 0.5 to 1.5
- w_qkv: bfloat16 [768, 2304], replicated, may hold values from -0.109375 to 0.109375
- rel_bias: float32 [32, 12], replicated, may hold values from -4 to 4
- w_self_out: bfloat16 [768, 768], replicated, may hold values from -0.875 to 0.875
- gain_cross: float32 [768], replicated, may hold values from 0.5 to 1.5
- w_cross_q: bfloat16 [768, 768], replicated, may hold values from -0.0546875 to 0.0546875
- w_cross_kv: bfloat16 [768, 1536], replicated, may hold values from -0.21875 to 0.21875
- w_cross_out: bfloat16 [768, 768], replicated, may hold values from -0.875 to 0.875
- gain_ff: float32 [768], replicated, may hold values from 0.5 to 1.5
- w_ff_in: bfloat16 [768, 3072], replicated, may hold values from -0.21875 to 0.21875
- w_ff_out: bfloat16 [3072, 768], replicated, may hold values from -0.109375 to 0.109375
- grad_out: bfloat16 [4, 4096, 768], P('dp', 'blk'), may hold values from -6 to 6
Outputs:
- dec_out: bfloat16 [4, 4096, 768], P('dp', 'blk')
- grad_dec: float32 [4, 4096, 768], P('dp', 'blk')
- grad_enc: float32 [4, 1024, 768], P('dp', 'blk')
- grad_gain_self: float32 [768], P('blk')
- grad_qkv: float32 [768, 2304], P('blk')
- grad_rel_bias: float32 [32, 12], P('blk')
- grad_self_out: float32 [768, 768], P('blk')
- grad_gain_cross: float32 [768], P('blk')
- grad_cross_q: float32 [768, 768], P('blk')
- grad_cross_kv: float32 [768, 1536], P('blk')
- grad_cross_out: float32 [768, 768], P('blk')
- grad_gain_ff: float32 [768], P('blk')
- grad_ff_in: float32 [768, 3072], P('blk')
- grad_ff_out: float32 [3072, 768], P('blk')
Inputs may be any that keep to these rules, and one draw needn't show every extreme that they name: `enc_question`: passages of 64 to 384 tokens lie end to end (the last one cut at the group's end); all tokens of a passage share its question; each passage has valid tokens from its start on, at least half of it; one question, drawn from the seed, holds the passages at the group's first, middle and last token, which are fully valid. `enc_valid`: padding lies at the end of each passage. `tgt_question`: each target names a question that has valid encoding tokens in its group; the first target of a group names the question that spans the group.
All inputs are finite; a program needn't handle non-finite values.
Results may differ from a plain program's by a relative error of at most 0.025.
Values may be sent and summed in bfloat16 or wider, within the bound.
No kernel may reach another device: no remote copies, remote signals or barrier semaphores. Data moves between devices by JAX's collectives and lax.ppermute only.
A program may use at most 192 MiB of HBM per device.

v0:
```python
import math

import jax
import jax.numpy as jnp
import numpy as np
from jax import lax
from jax.sharding import PartitionSpec as P

TLEN = 32


EPSILON = 1e-06
NEG_LARGE = -1e30
HIGHEST_PREC = lax.Precision.HIGHEST


def bucket_table(length, bucket_count):
    exact_count = bucket_count // 2
    bucket_ids = np.zeros((length, length), np.int32)
    for query_pos in range(length):
        for key_pos in range(length):
            distance = max(query_pos - key_pos, 0)
            if distance < exact_count:
                bucket_ids[query_pos, key_pos] = distance
            else:
                bucket_ids[query_pos, key_pos] = min(
                    bucket_count - 1,
                    exact_count
                    + int(
                        math.log(distance / exact_count)
                        / math.log(128.0 / exact_count)
                        * exact_count
                    ),
                )
    return bucket_ids


def rms_gain(values, gain):
    return values * lax.rsqrt(jnp.mean(values * values, axis=-1, keepdims=True) + EPSILON) * gain


def smooth_act(values):
    return jax.nn.gelu(values, approximate=True)


def local(
    dec_in,
    encodings,
    enc_question,
    enc_valid,
    tgt_question,
    gain_self,
    w_qkv,
    rel_bias,
    w_self_out,
    gain_cross,
    w_cross_q,
    w_cross_kv,
    w_cross_out,
    gain_ff,
    w_ff_in,
    w_ff_out,
    grad_out,
):
    hidden_in = dec_in[0].astype(jnp.float32)
    num_rows, model_width = hidden_in.shape
    bucket_count, num_heads = rel_bias.shape
    head_dim = model_width // num_heads
    tgt_len = TLEN
    targets = num_rows // tgt_len
    shard_rows = encodings.shape[1]
    cycle_size = lax.axis_size("blk")
    enc_rows = encodings[0]
    key_tags = jnp.where(enc_valid[0] == 1, enc_question[0], -1).astype(jnp.bfloat16)
    query_tags = jnp.repeat(tgt_question[0], tgt_len).astype(jnp.float32)
    bucket_ids = bucket_table(tgt_len, bucket_count)
    one_hot = jnp.asarray(
        (bucket_ids.reshape(-1)[:, None] == np.arange(bucket_count)[None, :]).astype(np.float32)
    )
    causal = jnp.asarray(np.tril(np.ones((tgt_len, tgt_len), bool)))
    self_bias = (
        jnp.dot(one_hot, rel_bias, precision=HIGHEST_PREC)
        .reshape(tgt_len, tgt_len, num_heads)
        .transpose(2, 0, 1)
    )
    norm_one, norm_one_back = jax.vjp(rms_gain, hidden_in, gain_self)
    act_one = norm_one.astype(jnp.bfloat16)
    qkv = jnp.dot(act_one, w_qkv, preferred_element_type=jnp.float32).astype(jnp.bfloat16)
    qkv = qkv.reshape(targets, tgt_len, 3, num_heads, head_dim)
    self_query, self_keys, self_vals = (qkv[:, :, 0], qkv[:, :, 1], qkv[:, :, 2])
    scores = (
        jnp.einsum("tqhd,tkhd->thqk", self_query, self_keys, preferred_element_type=jnp.float32)
        + self_bias[None]
    )
    masked = jnp.where(causal, scores, NEG_LARGE)
    exp_terms = jnp.where(causal, jnp.exp(masked - jnp.max(masked, -1, keepdims=True)), 0.0)
    self_probs = exp_terms / jnp.sum(exp_terms, -1, keepdims=True)
    probs_low = self_probs.astype(jnp.bfloat16)
    self_att = jnp.einsum(
        "thqk,tkhd->tqhd", probs_low, self_vals, preferred_element_type=jnp.float32
    )
    self_att = self_att.astype(jnp.bfloat16).reshape(num_rows, model_width)
    after_self = hidden_in + jnp.dot(self_att, w_self_out, preferred_element_type=jnp.float32)
    norm_two, norm_two_back = jax.vjp(rms_gain, after_self, gain_cross)
    act_two = norm_two.astype(jnp.bfloat16)
    cross_q = (
        jnp.dot(act_two, w_cross_q, preferred_element_type=jnp.float32)
        .astype(jnp.bfloat16)
        .reshape(num_rows, num_heads, head_dim)
    )
    kv_own = jnp.dot(enc_rows, w_cross_kv, preferred_element_type=jnp.float32).astype(jnp.bfloat16)
    start_state = (
        jnp.full((num_heads, num_rows), NEG_LARGE, jnp.float32),
        jnp.zeros((num_heads, num_rows), jnp.float32),
        jnp.zeros((num_rows, num_heads, head_dim), jnp.float32),
    )
    kv_piece = lax.all_gather(kv_own, "blk", axis=0, tiled=True)
    tag_piece = lax.all_gather(key_tags, "blk", axis=0, tiled=True)
    block_rows = math.gcd(kv_piece.shape[0], 512)
    num_blocks = kv_piece.shape[0] // block_rows

    def block_step(state, inputs):
        run_max, run_sum, weighted = state
        kv_block, tag_block = inputs
        kv_heads = kv_block.reshape(block_rows, 2, num_heads, head_dim)
        block_scores = jnp.einsum(
            "qhd,khd->hqk", cross_q, kv_heads[:, 0], preferred_element_type=jnp.float32
        )
        key_match = (query_tags[:, None] == tag_block.astype(jnp.float32)[None, :])[None]
        block_masked = jnp.where(key_match, block_scores, NEG_LARGE)
        new_max = jnp.maximum(run_max, jnp.max(block_masked, -1))
        block_weights = jnp.where(key_match, jnp.exp(block_masked - new_max[..., None]), 0.0)
        rescale = jnp.exp(run_max - new_max)
        new_sum = run_sum * rescale + jnp.sum(block_weights, -1)
        new_weighted = weighted * rescale.T[..., None] + jnp.einsum(
            "hqk,khd->qhd",
            block_weights.astype(jnp.bfloat16),
            kv_heads[:, 1],
            preferred_element_type=jnp.float32,
        )
        return ((new_max, new_sum, new_weighted), None)

    result, _ = lax.scan(
        block_step,
        start_state,
        (
            kv_piece.reshape(num_blocks, block_rows, 2 * model_width),
            tag_piece.reshape(num_blocks, block_rows),
        ),
    )
    run_max, run_sum, weighted = result
    cross_att = (weighted / run_sum.T[..., None]).astype(jnp.bfloat16)
    log_total = run_max + jnp.log(run_sum)
    cross_flat = cross_att.reshape(num_rows, model_width)
    after_cross = after_self + jnp.dot(cross_flat, w_cross_out, preferred_element_type=jnp.float32)
    norm_three, norm_three_back = jax.vjp(rms_gain, after_cross, gain_ff)
    act_three = norm_three.astype(jnp.bfloat16)
    pre_act = jnp.dot(act_three, w_ff_in, preferred_element_type=jnp.float32)
    gelu_out, gelu_back = jax.vjp(smooth_act, pre_act)
    ff_hidden = gelu_out.astype(jnp.bfloat16)
    output = after_cross + jnp.dot(ff_hidden, w_ff_out, preferred_element_type=jnp.float32)
    grad_top = grad_out[0].astype(jnp.float32)
    top_low = grad_top.astype(jnp.bfloat16)
    grad_w_two = jnp.einsum("rk,rd->kd", ff_hidden, top_low, preferred_element_type=jnp.float32)
    grad_hidden = jnp.einsum("rd,kd->rk", top_low, w_ff_out, preferred_element_type=jnp.float32)
    grad_pre = gelu_back(grad_hidden)[0].astype(jnp.bfloat16)
    grad_w_one = jnp.einsum("rd,rk->dk", act_three, grad_pre, preferred_element_type=jnp.float32)
    grad_act_three = jnp.einsum("rk,dk->rd", grad_pre, w_ff_in, preferred_element_type=jnp.float32)
    grad_norm_three, grad_gain_ff = norm_three_back(grad_act_three)
    grad_after_cross = grad_top + grad_norm_three
    cross_out_low = grad_after_cross.astype(jnp.bfloat16)
    grad_w_cross_out = jnp.einsum(
        "rk,rd->kd", cross_flat, cross_out_low, preferred_element_type=jnp.float32
    )
    grad_cross_att = (
        jnp.einsum("rd,kd->rk", cross_out_low, w_cross_out, preferred_element_type=jnp.float32)
        .astype(jnp.bfloat16)
        .reshape(num_rows, num_heads, head_dim)
    )
    row_dot = jnp.einsum(
        "qhd,qhd->hq", grad_cross_att, cross_att, preferred_element_type=jnp.float32
    )

    def block_grads(kv_block, tag_block):
        block_rows = kv_block.shape[0]
        kv_heads = kv_block.reshape(block_rows, 2, num_heads, head_dim)
        block_scores = jnp.einsum(
            "qhd,khd->hqk", cross_q, kv_heads[:, 0], preferred_element_type=jnp.float32
        )
        key_match = (query_tags[:, None] == tag_block.astype(jnp.float32)[None, :])[None]
        block_probs = jnp.where(
            key_match,
            jnp.exp(jnp.where(key_match, block_scores, NEG_LARGE) - log_total[..., None]),
            0.0,
        )
        grad_probs = jnp.einsum(
            "qhd,khd->hqk", grad_cross_att, kv_heads[:, 1], preferred_element_type=jnp.float32
        )
        grad_scores = (block_probs * (grad_probs - row_dot[..., None])).astype(jnp.bfloat16)
        return (grad_scores, block_probs.astype(jnp.bfloat16), kv_heads)

    def key_terms(grad_scores, probs_part):
        grad_key_block = jnp.einsum(
            "hqk,qhd->khd", grad_scores, cross_q, preferred_element_type=jnp.float32
        )
        grad_val_block = jnp.einsum(
            "hqk,qhd->khd", probs_part, grad_cross_att, preferred_element_type=jnp.float32
        )
        return jnp.stack([grad_key_block, grad_val_block], 1)

    back_state = (
        jnp.zeros((num_rows, num_heads, head_dim), jnp.float32),
        jnp.zeros((cycle_size * shard_rows, 2, num_heads, head_dim), jnp.float32),
    )
    kv_piece = lax.all_gather(kv_own, "blk", axis=0, tiled=True)
    tag_piece = lax.all_gather(key_tags, "blk", axis=0, tiled=True)
    attend_block_rows = math.gcd(kv_piece.shape[0], 512)
    num_blocks = kv_piece.shape[0] // attend_block_rows

    def block_back(state, inputs):
        grad_query, grad_keys = state
        block_index, kv_block, tag_block = inputs
        grad_scores, probs_part, kv_heads = block_grads(kv_block, tag_block)
        grad_query = grad_query + jnp.einsum(
            "hqk,khd->qhd", grad_scores, kv_heads[:, 0], preferred_element_type=jnp.float32
        )
        row_start = block_index * attend_block_rows
        grad_keys = lax.dynamic_update_slice_in_dim(
            grad_keys, key_terms(grad_scores, probs_part), row_start, 0
        )
        return ((grad_query, grad_keys), None)

    result, _ = lax.scan(
        block_back,
        back_state,
        (
            jnp.arange(num_blocks, dtype=jnp.int32),
            kv_piece.reshape(num_blocks, attend_block_rows, 2 * model_width),
            tag_piece.reshape(num_blocks, attend_block_rows),
        ),
    )
    grad_query, grad_keys = result
    grad_kv = lax.psum_scatter(
        grad_keys.reshape(cycle_size * shard_rows, 2 * model_width).astype(jnp.bfloat16),
        "blk",
        scatter_dimension=0,
        tiled=True,
    )
    grad_enc = jnp.einsum("ek,dk->ed", grad_kv, w_cross_kv, preferred_element_type=jnp.float32)
    grad_w_cross_kv = jnp.einsum("ed,ek->dk", enc_rows, grad_kv, preferred_element_type=jnp.float32)
    query_low = grad_query.reshape(num_rows, model_width).astype(jnp.bfloat16)
    grad_w_cross_q = jnp.einsum("rd,rk->dk", act_two, query_low, preferred_element_type=jnp.float32)
    grad_act_two = jnp.einsum("rk,dk->rd", query_low, w_cross_q, preferred_element_type=jnp.float32)
    grad_norm_two, grad_gain_cross = norm_two_back(grad_act_two)
    grad_after_self = grad_after_cross + grad_norm_two
    self_out_low = grad_after_self.astype(jnp.bfloat16)
    grad_w_self_out = jnp.einsum(
        "rk,rd->kd", self_att, self_out_low, preferred_element_type=jnp.float32
    )
    grad_self_att = (
        jnp.einsum("rd,kd->rk", self_out_low, w_self_out, preferred_element_type=jnp.float32)
        .astype(jnp.bfloat16)
        .reshape(targets, tgt_len, num_heads, head_dim)
    )
    grad_self_probs = jnp.einsum(
        "tqhd,tkhd->thqk", grad_self_att, self_vals, preferred_element_type=jnp.float32
    )
    grad_self_scores = (
        self_probs * (grad_self_probs - jnp.sum(self_probs * grad_self_probs, -1, keepdims=True))
    ).astype(jnp.bfloat16)
    grad_self_query = jnp.einsum(
        "thqk,tkhd->tqhd", grad_self_scores, self_keys, preferred_element_type=jnp.float32
    )
    grad_self_keys = jnp.einsum(
        "thqk,tqhd->tkhd", grad_self_scores, self_query, preferred_element_type=jnp.float32
    )
    grad_self_vals = jnp.einsum(
        "thqk,tqhd->tkhd", probs_low, grad_self_att, preferred_element_type=jnp.float32
    )
    grad_qkv_rows = (
        jnp.stack([grad_self_query, grad_self_keys, grad_self_vals], 2)
        .reshape(num_rows, 3 * model_width)
        .astype(jnp.bfloat16)
    )
    bias_terms = (
        jnp.sum(grad_self_scores.astype(jnp.float32), 0)
        .transpose(1, 2, 0)
        .reshape(tgt_len * tgt_len, num_heads)
    )
    grad_bias = jnp.dot(one_hot.T, bias_terms, precision=HIGHEST_PREC)
    grad_w_qkv = jnp.einsum("rd,rk->dk", act_one, grad_qkv_rows, preferred_element_type=jnp.float32)
    grad_act_one = jnp.einsum("rk,dk->rd", grad_qkv_rows, w_qkv, preferred_element_type=jnp.float32)
    grad_norm_one, grad_gain_self = norm_one_back(grad_act_one)
    grad_input = grad_after_self + grad_norm_one
    shares = (
        lax.psum_scatter(
            grad_gain_self.astype(jnp.bfloat16), "blk", scatter_dimension=0, tiled=True
        ).astype(jnp.float32),
        lax.psum_scatter(
            grad_w_qkv.astype(jnp.bfloat16), "blk", scatter_dimension=0, tiled=True
        ).astype(jnp.float32),
        lax.psum_scatter(
            grad_bias.astype(jnp.bfloat16), "blk", scatter_dimension=0, tiled=True
        ).astype(jnp.float32),
        lax.psum_scatter(
            grad_w_self_out.astype(jnp.bfloat16), "blk", scatter_dimension=0, tiled=True
        ).astype(jnp.float32),
        lax.psum_scatter(
            grad_gain_cross.astype(jnp.bfloat16), "blk", scatter_dimension=0, tiled=True
        ).astype(jnp.float32),
        lax.psum_scatter(
            grad_w_cross_q.astype(jnp.bfloat16), "blk", scatter_dimension=0, tiled=True
        ).astype(jnp.float32),
        lax.psum_scatter(
            grad_w_cross_kv.astype(jnp.bfloat16), "blk", scatter_dimension=0, tiled=True
        ).astype(jnp.float32),
        lax.psum_scatter(
            grad_w_cross_out.astype(jnp.bfloat16), "blk", scatter_dimension=0, tiled=True
        ).astype(jnp.float32),
        lax.psum_scatter(
            grad_gain_ff.astype(jnp.bfloat16), "blk", scatter_dimension=0, tiled=True
        ).astype(jnp.float32),
        lax.psum_scatter(
            grad_w_one.astype(jnp.bfloat16), "blk", scatter_dimension=0, tiled=True
        ).astype(jnp.float32),
        lax.psum_scatter(
            grad_w_two.astype(jnp.bfloat16), "blk", scatter_dimension=0, tiled=True
        ).astype(jnp.float32),
    )
    totals = (
        lax.psum(shares[0].astype(jnp.bfloat16), "dp").astype(jnp.float32),
        lax.psum(shares[1].astype(jnp.bfloat16), "dp").astype(jnp.float32),
        lax.psum(shares[2].astype(jnp.bfloat16), "dp").astype(jnp.float32),
        lax.psum(shares[3].astype(jnp.bfloat16), "dp").astype(jnp.float32),
        lax.psum(shares[4].astype(jnp.bfloat16), "dp").astype(jnp.float32),
        lax.psum(shares[5].astype(jnp.bfloat16), "dp").astype(jnp.float32),
        lax.psum(shares[6].astype(jnp.bfloat16), "dp").astype(jnp.float32),
        lax.psum(shares[7].astype(jnp.bfloat16), "dp").astype(jnp.float32),
        lax.psum(shares[8].astype(jnp.bfloat16), "dp").astype(jnp.float32),
        lax.psum(shares[9].astype(jnp.bfloat16), "dp").astype(jnp.float32),
        lax.psum(shares[10].astype(jnp.bfloat16), "dp").astype(jnp.float32),
    )
    return (
        output.astype(jnp.bfloat16)[None],
        grad_input[None],
        grad_enc[None],
        totals[0],
        totals[1],
        totals[2],
        totals[3],
        totals[4],
        totals[5],
        totals[6],
        totals[7],
        totals[8],
        totals[9],
        totals[10],
    )


def solution(mesh):
    return jax.shard_map(
        local,
        mesh=mesh,
        in_specs=(
            P("dp", "blk", None),
            P("dp", "blk", None),
            P("dp", "blk"),
            P("dp", "blk"),
            P("dp", "blk"),
            P(),
            P(),
            P(),
            P(),
            P(),
            P(),
            P(),
            P(),
            P(),
            P(),
            P(),
            P("dp", "blk", None),
        ),
        out_specs=(
            P("dp", "blk", None),
            P("dp", "blk", None),
            P("dp", "blk", None),
            P("blk"),
            P("blk", None),
            P("blk", None),
            P("blk", None),
            P("blk"),
            P("blk", None),
            P("blk", None),
            P("blk", None),
            P("blk"),
            P("blk", None),
            P("blk", None),
        ),
        check_vma=False,
    )
```

profile of v0, /device:TPU:1, one launch (start us, length us, event | category | flops | bytes accessed | tf_op | source)
XLA Modules:
  0.0 913.0 jit_solution(16752539948027225851)
XLA Ops:
  10.6 17.9 %all-gather = bf16[1,1024]{1,0:T(2,128)(2,1)S(1)} all-gather(bf16[1,128]{1,0:T(2,128)(2,1)S(1)} %fusion.92), channel_id=2, replica_groups=mesh['dp'=4,'blk'=8] {'blk'}, dimensions={1}, use_global_device_ids=true | all-gather | bytes 2304 | tf_op jit(solution)/shard_map/all_gather | solution.py:118
  41.3 8.2 reshape.233
  77.8 30.7 %while.28 = (s32[]{:T(128)}, f32[12,512]{1,0:T(8,128)}, f32[12,512]{1,0:T(8,128)}, f32[512,12,64]{0,2,1:T(8,128)}, bf16[2,512]{1,0:T(2,128)(2,1)S(1)}, /*index=5...) while((s32[]{:T(128)}, f32[12,512]{1,0:T(8,128)}, ...), condition=%wide.region_7.8_spmd.clone, body=%wide.region_4.7_spmd.clone.sunk | while | flops 838242816 | bytes 52164424 | solution.py:143
  117.4 6.6 fusion.38
  137.5 60.1 %while.29 = (s32[]{:T(128)}, f32[512,12,64]{0,2,1:T(8,128)}, bf16[1024,2,12,64]{0,3,2,1:T(8,128)(2,1)}, bf16[2,512,1536]{1,2,0:T(8,128)(2,1)}, bf16[2,512]{1,0:T...) while((s32[]{:T(128)}, f32[512,12,64]{0,2,1:T(8,128)}, ...), condition=%wide.region_11.12_spmd.clone, body=%wide.region_10.11_spmd.clone.sunk | while | flops 2048918016 | bytes 118266024 | solution.py:233
  142.1 6.3 fusion.166
  148.4 6.3 fusion.168
  154.7 7.2 fusion.167
  172.1 6.3 fusion.166
  184.8 7.2 fusion.167
  202.6 74.7 %reduce-scatter.26.cloned.1.call-done = bf16[128,1536]{1,0:T(8,128)(2,1)} async-done(((bf16[1024,1536]{1,0:T(8,128)(2,1)}), bf16[128,1536]{1,0:T(8,128)(2,1)}) %reduce-scatter.26.cloned.1.call-update) | async-done | bytes 393232
  307.5 6.7 multiply_reduce_fusion
  329.6 8.4 convert_element_type.260
  344.1 8.5 convolution_convert_fusion
  353.3 7.3 convolution_convert_fusion.1
  373.6 28.7 %all-reduce.4 = (bf16[32,12]{0,1:T(8,128)(2,1)S(1)}, bf16[768]{0:T(1024)(128)(2,1)}, bf16[768]{0:T(1024)(128)(2,1)}, bf16[768]{0:T(1024)(128)(2,1)}) all-reduce(bf16[32,12]{0,1:T(8,128)(2,1)S(1)} %fusion.68, bf16[768]{0:T(1024)(128)(2,1)} %get-tuple-element.326, ...), channel_id=6, replica_groups=mesh['dp'=4,'blk'=8] {'blk'}, use_global_device_ids=true, to_apply=%region_22.23.clone | all-reduce | flops 2688 | bytes 10752
  406.2 13.8 %all-reduce.5 = (bf16[4,12]{0,1:T(8,128)(2,1)S(1)}, bf16[96]{0:T(256)(128)(2,1)}, bf16[96]{0:T(256)(128)(2,1)}, bf16[96]{0:T(256)(128)(2,1)}) all-reduce(bf16[4,12]{0,1:T(8,128)(2,1)S(1)} %constant_dynamic-slice_fusion.2, bf16[96]{0:T(256)(128)(2,1)} %dynamic-slice.1, ...), channel_id=1, replica_groups=mesh['dp'=4,'blk'=8] {'dp'}, use_global_device_ids=true, to_apply=%region_23.24 | all-reduce | flops 336 | bytes 1344 | tf_op jit(solution)/shard_map/psum | solution.py:333
  430.4 55.2 %reduce-scatter.18.cloned.1.call-done = bf16[96,768]{1,0:T(8,128)(2,1)} async-done(((bf16[768,768]{1,0:T(8,128)(2,1)}), bf16[96,768]{1,0:T(8,128)(2,1)}) %reduce-scatter.18.cloned.1.call-update) | async-done | bytes 147472 | tf_op jit(solution)/shard_map/reduce_scatter | solution.py:311
  485.5 67.0 %reduce-scatter.16.cloned.1.call-done = bf16[96,768]{1,0:T(8,128)(2,1)} async-done(((bf16[768,768]{1,0:T(8,128)(2,1)}), bf16[96,768]{1,0:T(8,128)(2,1)}) %reduce-scatter.16.cloned.1.call-update) | async-done | bytes 147472 | tf_op jit(solution)/shard_map/reduce_scatter | solution.py:305
  552.6 83.1 %reduce-scatter.14.cloned.1.call-done = bf16[96,2304]{1,0:T(8,128)(2,1)} async-done(((bf16[768,2304]{1,0:T(8,128)(2,1)}), bf16[96,2304]{1,0:T(8,128)(2,1)}) %reduce-scatter.14.cloned.1.call-update) | async-done | bytes 442384 | tf_op jit(solution)/shard_map/reduce_scatter | solution.py:299
  635.7 98.8 %reduce-scatter.24.cloned.1.call-done = bf16[384,768]{1,0:T(8,128)(2,1)} async-done(((bf16[3072,768]{1,0:T(8,128)(2,1)}), bf16[384,768]{1,0:T(8,128)(2,1)}) %reduce-scatter.24.cloned.1.call-update) | async-done | bytes 589840 | tf_op jit(solution)/shard_map/reduce_scatter | solution.py:326
  734.5 98.8 %reduce-scatter.22.cloned.1.call-done = bf16[96,3072]{1,0:T(8,128)(2,1)} async-done(((bf16[768,3072]{1,0:T(8,128)(2,1)}), bf16[96,3072]{1,0:T(8,128)(2,1)}) %reduce-scatter.22.cloned.1.call-update) | async-done | bytes 589840 | tf_op jit(solution)/shard_map/reduce_scatter | solution.py:323
  833.4 9.4 %fusion.63 = bf16[1,512,768]{2,1,0:T(8,128)(2,1)} fusion(f32[512,768]{1,0:T(8,128)} %copy-done.13, bf16[3072,768]{1,0:T(8,128)(2,1)} %param.38, f32[512,3072]{1,0:T(8,128)} %copy-done.22), kind=kOutput, calls=%fused_computation.123 | convolution fusion | flops 2430861312 | bytes 13369344 | tf_op jit(solution)/shard_map/dot_general | solution.py:161
  844.4 50.1 %all-reduce.9.cloned.1.call-done = (bf16[96,1536]{0,1:T(8,128)(2,1)}, bf16[96,2304]{1,0:T(8,128)(2,1)}, bf16[96,768]{1,0:T(8,128)(2,1)}, bf16[96,768]{1,0:T(8,12...) async-done(((bf16[96,1536]{0,1:T(8,128)(2,1)}, bf16[96,2304]{1,0:T(8,128)(2,1)}, bf16[96,768]{1,0:T(8,128)(2,1)}, ...) | async-done | bytes 2359312 | tf_op jit(solution)/shard_map/psum | solution.py:337
  (327 shorter events, 218.1 us)
Async XLA Ops:
  7.2 29.4 %copy-start = (bf16[768,2304]{1,0:T(8,128)(2,1)S(1)}, bf16[768,2304]{1,0:T(8,128)(2,1)}, u32[]{:S(2)}) copy-start(bf16[768,2304]{1,0:T(8,128)(2,1)} %param.29) | copy-start | bytes 10616836
  7.2 29.4 %copy-start.59 = (f32[768]{0:T(1024)S(1)}, f32[768]{0:T(1024)}, u32[]{:S(2)}) copy-start(f32[768]{0:T(1024)} %param.28) | copy-start | bytes 9220
  7.2 65.9 %all-gather.3.cloned.1.call-start = ((), (), s32[]{:S(2)}) async-start(), calls=%async_computation.8 | async-start | bytes 3538944 | tf_op jit(solution)/shard_map/all_gather | solution.py:117
  10.4 266.9 %reduce-scatter.26.cloned.1.call-start = ((), (), s32[]{:S(2)}) async-start(), calls=%async_computation.15 | async-start | bytes 3538944
  114.2 13.1 %copy-start.13 = (f32[512,768]{1,0:T(8,128)}, f32[512,768]{1,0:T(8,128)S(1)}, u32[]{:S(2)}) copy-start(f32[512,768]{1,0:T(8,128)S(1)} %get-tuple-element.395) | copy-start | bytes 4718596
  114.2 13.1 %copy-start.46 = (f32[512]{0:T(512)}, f32[512]{0:T(512)S(1)}, u32[]{:S(2)}) copy-start(f32[512]{0:T(512)S(1)} %fusion.91) | copy-start | bytes 6148
  117.3 6.6 copy-start.22
  154.7 7.3 copy-start.4
  184.8 7.3 copy-start.4
  202.4 226.1 %reduce-scatter.28.cloned.1.call-start = ((), (), s32[]{:S(2)}) async-start(), calls=%async_computation.16 | async-start | bytes 2654208
  284.9 145.5 %reduce-scatter.20.cloned.1.call-start = ((), (), s32[]{:S(2)}) async-start(), calls=%async_computation.12 | async-start | bytes 1327104 | tf_op jit(solution)/shard_map/reduce_scatter | solution.py:317
  288.4 197.1 %reduce-scatter.18.cloned.1.call-start = ((), (), s32[]{:S(2)}) async-start(), calls=%async_computation.11 | async-start | bytes 1327104 | tf_op jit(solution)/shard_map/reduce_scatter | solution.py:311
  293.0 259.5 %reduce-scatter.16.cloned.1.call-start = ((), (), s32[]{:S(2)}) async-start(), calls=%async_computation.10 | async-start | bytes 1327104 | tf_op jit(solution)/shard_map/reduce_scatter | solution.py:305
  314.2 321.5 %reduce-scatter.14.cloned.1.call-start = ((), (), s32[]{:S(2)}) async-start(), calls=%async_computation.9 | async-start | bytes 3981312 | tf_op jit(solution)/shard_map/reduce_scatter | solution.py:299
  329.6 8.4 copy-start.56
  329.6 8.4 copy-start.60
  344.1 390.5 %reduce-scatter.24.cloned.1.call-start = ((), (), s32[]{:S(2)}) async-start(), calls=%async_computation.14 | async-start | bytes 5308416 | tf_op jit(solution)/shard_map/reduce_scatter | solution.py:326
  352.6 480.7 %reduce-scatter.22.cloned.1.call-start = ((), (), s32[]{:S(2)}) async-start(), calls=%async_computation.13 | async-start | bytes 5308416 | tf_op jit(solution)/shard_map/reduce_scatter | solution.py:323
  360.6 534.0 %all-reduce.9.cloned.1.call-start = ((), (), s32[]{:S(2)}) async-start(), calls=%async_computation.17 | async-start | bytes 4915200 | tf_op jit(solution)/shard_map/psum | solution.py:337
  367.9 56.2 %copy-start.52 = (f32[512]{0:T(512)S(1)}, f32[512]{0:T(512)}, u32[]{:S(2)}) copy-start(f32[512]{0:T(512)} %copy-done.51) | copy-start | bytes 6148
  833.4 9.4 %copy-start.20 = (bf16[768,1536]{1,0:T(8,128)(2,1)S(1)}, bf16[768,1536]{1,0:T(8,128)(2,1)}, u32[]{:S(2)}) copy-start(bf16[768,1536]{1,0:T(8,128)(2,1)} %param.34) | copy-start | bytes 7077892
  833.4 9.4 %copy-start.31 = (bf16[128,1536]{1,0:T(8,128)(2,1)S(1)}, bf16[128,1536]{1,0:T(8,128)(2,1)}, u32[]{:S(2)}) copy-start(bf16[128,1536]{1,0:T(8,128)(2,1)} %reduce-scatter.26.cloned.1.call-done) | copy-start | bytes 1179652
  896.5 7.0 copy-start.35
  898.2 6.5 copy-start.34
  (76 other events, 201.1 us)
Sparse Core Ops, SparseCore 0:
  10.8 61.6 all-gather.2
  202.5 74.7 reduce-scatter.25
  285.0 67.6 reduce-scatter.27
  355.9 62.5 reduce-scatter.19
  422.4 63.1 reduce-scatter.17
  489.4 63.1 reduce-scatter.15
  556.2 79.4 reduce-scatter.13
  639.4 95.1 reduce-scatter.23
  738.2 95.0 reduce-scatter.21
  836.6 57.8 all-reduce.8
where the time goes:
time: 924 us; the launch traced here: 913 us
  waiting for transfers between devices  528 us (57%)
  matrix products  159 us (17%)
  local copies, waits for them, and re-layouts  96.5 us (10%)
  blocking collectives  60.3 us (7%)
  other arithmetic  49.8 us (5%)
  between operations  16.5 us (2%)
    reduce_scatter x1, waiting for transfers between devices, local(): lax.psum_scatter(grad_w_two.astype(jnp.bfloat16), 'blk', scatter_dimensio...  98.8 us
    reduce_scatter x1, waiting for transfers between devices, local(): lax.psum_scatter(grad_w_one.astype(jnp.bfloat16), 'blk', scatter_dimensio...  98.8 us
    reduce_scatter x1, waiting for transfers between devices, local(): lax.psum_scatter(grad_w_qkv.astype(jnp.bfloat16), 'blk', scatter_dimensio...  83.1 us
    unnamed x12, waiting for transfers between devices  74.9 us
    reduce_scatter x1, waiting for transfers between devices, local(): lax.psum_scatter(grad_w_self_out.astype(jnp.bfloat16), 'blk', scatter_dim...  67 us
    reduce_scatter x1, waiting for transfers between devices, local(): lax.psum_scatter(grad_w_cross_q.astype(jnp.bfloat16), 'blk', scatter_dime...  55.2 us
    psum x1, waiting for transfers between devices, local(): lax.psum(shares[6].astype(jnp.bfloat16), 'dp').astype(jnp.float32)  50.1 us
    unnamed x123, local copies, waits for them, and re-layouts  33.6 us
  transfers between devices with their start and end apart: 10, of which 7 were waited for; matrix products, arithmetic and copies ran while one was open for 16% of the time, Pallas kernels for 0%

commit v1 on v0

v1 whole, which is shorter than its diff:
```python
import functools
import math

import jax
import jax.numpy as jnp
import numpy as np
from jax import lax
from jax.experimental import pallas as pl
from jax.experimental.pallas import tpu as pltpu
from jax.sharding import PartitionSpec as P

TLEN = 32
EPSILON = 1e-06
NEG_LARGE = -1e30
GROUP = 128
LOG2E = 1.4426950408889634
BF = jnp.bfloat16
F32 = jnp.float32
VMEM = pl.BlockSpec(memory_space=pltpu.VMEM)
SMEM = pl.BlockSpec(memory_space=pltpu.SMEM)
ANY = pl.BlockSpec(memory_space=pl.ANY)
MIB = 2**20


def bucket_of(distance, bucket_count):
    exact_count = bucket_count // 2
    if distance < exact_count:
        return distance
    scaled = math.log(distance / exact_count) / math.log(128.0 / exact_count) * exact_count
    return min(bucket_count - 1, exact_count + int(scaled))


def bucket_ids(bucket_count):
    ids = np.full((GROUP, GROUP), -1, np.int32)
    for row in range(GROUP):
        first = row - row % TLEN
        for col in range(first, row + 1):
            ids[row, col] = bucket_of(row - col, bucket_count)
    return ids


def dot_nn(a, b):
    return jnp.dot(a, b, preferred_element_type=F32)


def dot_nt(a, b):
    return lax.dot_general(a, b, (((1,), (1,)), ((), ())), preferred_element_type=F32)


def dot_tn(a, b):
    return lax.dot_general(a, b, (((0,), (0,)), ((), ())), preferred_element_type=F32)


def inv_rms(v):
    return lax.rsqrt(jnp.mean(v * v, axis=-1, keepdims=True) + EPSILON)


def rms_back(dy, v, gain):
    r = inv_rms(v)
    vr = v * r
    dg = dy * gain
    dv = r * (dg - vr * jnp.mean(dg * vr, axis=-1, keepdims=True))
    return dv, jnp.sum(dy * vr, axis=0, keepdims=True)


def half_masks(rows):
    lane = lax.broadcasted_iota(jnp.int32, (rows, 128), 1)
    low = (lane < 64).astype(F32)
    return low.astype(BF), (1.0 - low).astype(BF)


def chunk_place(chunk, blk, bits):
    rel = jnp.bitwise_xor(chunk, blk)
    place = jnp.int32(0)
    for bit in bits:
        place = place * 2 + jnp.where(jnp.bitwise_and(rel, bit) != 0, 1, 0)
    return place


def query_block(rows, tokens):
    return max(GROUP, min(rows, rows * 1024 // tokens))


def store_chunks(ref, value, col, blk, bits, chunks):
    rows = value.shape[0] // chunks
    for c in range(chunks):
        ref[chunk_place(c, blk, bits), :, col : col + value.shape[1]] = value[
            c * rows : (c + 1) * rows, :
        ].astype(BF)


def call(body, out_shape, in_specs, out_specs, scratch=(), limit=56, flops=0, nbytes=0):
    return pl.pallas_call(
        body,
        out_shape=out_shape,
        in_specs=in_specs,
        out_specs=out_specs,
        scratch_shapes=list(scratch),
        compiler_params=pltpu.CompilerParams(vmem_limit_bytes=limit * MIB),
        cost_estimate=pl.CostEstimate(flops=flops, bytes_accessed=nbytes, transcendentals=0),
    )


def self_forward(x, gain_self, w_qkv, rel_bias, w_self_out, gain_cross, w_cross_q):
    rows, width = x.shape
    bucket_count, heads = rel_bias.shape
    pairs = heads // 2
    groups = rows // GROUP
    ids = bucket_ids(bucket_count)
    used = sorted(set(ids[ids >= 0].tolist()))

    def body(
        x_ref, gs_ref, wqkv_ref, ids_ref, rb_ref, wso_ref, gc_ref, wcq_ref,
        a1_ref, qkv_ref, p1_ref, o1_ref, h1_ref, a2_ref, cq_ref, bias,
    ):
        xf = x_ref[...].astype(F32)
        a1 = (xf * inv_rms(xf) * gs_ref[...]).astype(BF)
        a1_ref[...] = a1
        qkv_ref[...] = dot_nn(a1, wqkv_ref[...]).astype(BF)
        idv = ids_ref[...]

        def make_bias(h, carry):
            val = jnp.full((GROUP, GROUP), NEG_LARGE, F32)
            for b in used:
                val = jnp.where(idv == b, rb_ref[b, h], val)
            bias[h] = val
            return carry

        lax.fori_loop(0, heads, make_bias, 0)
        m0, m1 = half_masks(GROUP)

        def attend(g, carry):
            at = pl.ds(pl.multiple_of(g * GROUP, GROUP), GROUP)
            for pair in range(pairs):
                lo = pair * 128
                q = qkv_ref[at, lo : lo + 128]
                k = qkv_ref[at, width + lo : width + lo + 128]
                v = qkv_ref[at, 2 * width + lo : 2 * width + lo + 128]
                s = dot_nt(jnp.concatenate([q * m0, q * m1], 0), k)
                s = s + jnp.concatenate([bias[2 * pair], bias[2 * pair + 1]], 0)
                e = jnp.exp(s - jnp.max(s, -1, keepdims=True))
                p = (e / jnp.sum(e, -1, keepdims=True)).astype(BF)
                p1_ref[g, pair] = p
                o = dot_nn(
                    jnp.concatenate([p[:GROUP], p[GROUP:]], 1),
                    jnp.concatenate([v * m0, v * m1], 0),
                )
                o1_ref[at, lo : lo + 128] = o.astype(BF)
            return carry

        lax.fori_loop(0, groups, attend, 0)
        h1 = x_ref[...].astype(F32) + dot_nn(o1_ref[...], wso_ref[...])
        h1_ref[...] = h1
        a2 = (h1 * inv_rms(h1) * gc_ref[...]).astype(BF)
        a2_ref[...] = a2
        cq_ref[...] = dot_nn(a2, wcq_ref[...]).astype(BF)

    sds = jax.ShapeDtypeStruct
    return call(
        body,
        (
            sds((rows, width), BF),
            sds((rows, 3 * width), BF),
            sds((groups, pairs, 2 * GROUP, GROUP), BF),
            sds((rows, width), BF),
            sds((rows, width), F32),
            sds((rows, width), BF),
            sds((rows, width), BF),
        ),
        [VMEM, VMEM, VMEM, VMEM, SMEM, VMEM, VMEM, VMEM],
        (VMEM,) * 7,
        [pltpu.VMEM((heads, GROUP, GROUP), F32)],
        flops=12 * 10**9,
        nbytes=16 * 10**6,
    )(
        x, gain_self.reshape(1, width), w_qkv, jnp.asarray(ids), rel_bias, w_self_out,
        gain_cross.reshape(1, width), w_cross_q,
    )


def cross_forward(gathered, shard_rows, tgt_question, cq, h1, w_cross_kv, w_cross_out, gain_ff):
    rows, width = cq.shape
    pairs = width // 128
    pieces, piece_rows, _ = gathered.shape
    tokens = pieces * shard_rows
    targets = rows // TLEN
    block_rows = query_block(rows, tokens)
    blocks = rows // block_rows
    steps = pairs * blocks

    def body(
        enc_ref, tq_ref, cq_ref, h1_ref, wkv_ref, wco_ref, gf_ref,
        kv_ref, e_ref, inv_ref, o2_ref, h2_ref, a3_ref,
        enc, kfeat, qfeat, ebuf, sem,
    ):
        lane = lax.rem(lax.broadcasted_iota(jnp.int32, (shard_rows, 128), 1), 64).astype(F32)
        for piece in range(pieces):
            at = slice(piece * shard_rows, (piece + 1) * shard_rows)
            enc[at, :] = enc_ref[piece, :shard_rows, :]
            tag = enc_ref[piece, shard_rows : shard_rows + 1, :shard_rows].astype(F32)
            tag = jnp.transpose(jnp.broadcast_to(tag, (128, shard_rows)))
            kfeat[at, :] = jnp.where(tag == lane, 0.0, NEG_LARGE).astype(BF)
        lane_t = lax.rem(lax.broadcasted_iota(jnp.int32, (TLEN, 128), 1), 64)
        for t in range(targets):
            qfeat[t * TLEN : (t + 1) * TLEN, :] = jnp.where(lane_t == tq_ref[t], 1.0, 0.0).astype(BF)
        kv_ref[...] = dot_nn(enc[...], wkv_ref[...]).astype(BF)
        q0, q1 = half_masks(block_rows)
        k0, k1 = half_masks(tokens)
        qmask, kmask = (q0, q1), (k0, k1)
        low = lax.broadcasted_iota(jnp.int32, (block_rows, 128), 1) < 64

        def out_copy(slot, step):
            pair, block = step // blocks, lax.rem(step, blocks)
            return pltpu.make_async_copy(
                ebuf.at[slot],
                e_ref.at[pl.ds(2 * pair, 2), pl.ds(block * block_rows, block_rows)],
                sem.at[slot],
            )

        def attend(step, carry):
            slot = lax.rem(step, 2)
            pair, block = step // blocks, lax.rem(step, blocks)
            lo = pl.multiple_of(pair * 128, 128)
            at = pl.ds(pl.multiple_of(block * block_rows, block_rows), block_rows)

            @pl.when(step >= 2)
            def _():
                out_copy(slot, step - 2).wait()

            q = cq_ref[at, pl.ds(lo, 128)]
            k = kv_ref[:, pl.ds(lo, 128)]
            v = kv_ref[:, pl.ds(width + lo, 128)]
            outs = []
            for h in range(2):
                qa = q * qmask[h] + qfeat[at, :] * qmask[1 - h]
                ka = k * kmask[h] + kfeat[...] * kmask[1 - h]
                s = dot_nt(qa, ka)
                top = jnp.max(s, -1, keepdims=True)
                e = jnp.exp(s - top).astype(BF)
                ebuf[slot, h] = e
                outs.append(dot_nn(e, v * kmask[h] + kmask[1 - h]))
            out_copy(slot, step).start()
            total = jnp.where(low, pltpu.roll(outs[0], 64, 1), pltpu.roll(outs[1], 64, 1))
            inv = 1.0 / total
            inv_ref[at, pl.ds(lo, 128)] = inv
            o2_ref[at, pl.ds(lo, 128)] = (jnp.where(low, outs[0], outs[1]) * inv).astype(BF)
            return carry

        lax.fori_loop(0, steps, attend, 0)
        h2 = h1_ref[...] + dot_nn(o2_ref[...], wco_ref[...])
        h2_ref[...] = h2
        a3_ref[...] = (h2 * inv_rms(h2) * gf_ref[...]).astype(BF)
        for step in range(max(0, steps - 2), steps):
            out_copy(step % 2, jnp.int32(step)).wait()

    sds = jax.ShapeDtypeStruct
    return call(
        body,
        (
            sds((tokens, 2 * width), BF),
            sds((2 * pairs, rows, tokens), BF),
            sds((rows, width), F32),
            sds((rows, width), BF),
            sds((rows, width), F32),
            sds((rows, width), BF),
        ),
        [VMEM, SMEM, VMEM, VMEM, VMEM, VMEM, VMEM],
        (VMEM, ANY, VMEM, VMEM, VMEM, VMEM),
        [
            pltpu.VMEM((tokens, width), BF),
            pltpu.VMEM((tokens, 128), BF),
            pltpu.VMEM((rows, 128), BF),
            pltpu.VMEM((2, 2, block_rows, tokens), BF),
            pltpu.SemaphoreType.DMA((2,)),
        ],
        flops=16 * 10**9,
        nbytes=30 * 10**6,
    )(gathered, tgt_question, cq, h1, w_cross_kv, w_cross_out, gain_ff.reshape(1, width))


def feed_forward(place, a3, h2, gain_ff, gy, w_ff_in, w_ff_out, bits, chunks):
    rows, width = a3.shape
    hidden = w_ff_in.shape[1]
    tile = width
    steps = hidden // tile
    part = width // chunks
    half_steps = steps // 2
    half = width // 2
    cols = hidden
    sub = hidden // width
    per_tile = chunks * tile // hidden
    scale = math.sqrt(2.0 / math.pi)

    def body(
        place_ref, a3_ref, h2_ref, gf_ref, gy_ref, w1_ref, w2_ref,
        out_ref, dh2_ref, gain_ref, keep_ref, send_ref,
        acc_out, acc_back,
    ):
        core, blk = place_ref[0], place_ref[1]
        step = pl.program_id(0)

        @pl.when(step == 0)
        def _():
            acc_out[...] = jnp.zeros_like(acc_out)
            acc_back[...] = jnp.zeros_like(acc_back)

        a3v = a3_ref[...]
        gyv = gy_ref[...]
        pre = dot_nn(a3v, w1_ref[...])
        dhid = dot_nt(gyv, w2_ref[...])
        sq = pre * pre
        t = jnp.tanh(scale * pre * (1.0 + 0.044715 * sq))
        hid = (0.5 * pre * (1.0 + t)).astype(BF)
        slope = 0.5 * (1.0 + t) + 0.5 * pre * (1.0 - t * t) * (scale * (1.0 + 0.134145 * sq))
        dpre = (dhid * slope).astype(BF)
        acc_out[...] += dot_nn(hid, w2_ref[...])
        acc_back[...] += dot_nt(dpre, w1_ref[...])
        g_in = dot_tn(a3v, dpre)
        mine = step // half_steps == core
        col = pl.multiple_of(lax.rem(step, half_steps) * tile, tile)
        for wanted, ref in ((True, keep_ref), (False, send_ref)):

            @pl.when(mine == wanted)
            def _():
                for c in range(chunks):
                    ref[chunk_place(c, blk, bits), :, pl.ds(col, tile)] = g_in[
                        c * part : (c + 1) * part, :
                    ].astype(BF)

        g_out = dot_tn(hid, gyv)
        swap = core == 1
        low_half, high_half = g_out[:, :half], g_out[:, half:]
        g_keep = jnp.where(swap, high_half, low_half).astype(BF)
        g_send = jnp.where(swap, low_half, high_half).astype(BF)
        for value, ref in ((g_keep, keep_ref), (g_send, send_ref)):
            for i in range(per_tile):
                for j in range(sub):
                    first = (i * sub + j) * part
                    ref[
                        chunk_place(step * per_tile + i, blk, bits),
                        :,
                        hidden // 2 + j * half : hidden // 2 + (j + 1) * half,
                    ] = value[first : first + part, :]

        @pl.when(step == steps - 1)
        def _():
            h2v = h2_ref[...]
            out_ref[...] = (h2v + acc_out[...]).astype(BF)
            dv, dgain = rms_back(acc_back[...], h2v, gf_ref[...])
            dh2_ref[...] = gyv.astype(F32) + dv
            gain_ref[...] = dgain

    sds = jax.ShapeDtypeStruct
    whole = lambda *shape: pl.BlockSpec(shape, lambda s, *_: (0,) * len(shape))
    return pl.pallas_call(
        body,
        out_shape=(
            sds((rows, width), BF),
            sds((rows, width), F32),
            sds((1, width), F32),
            sds((chunks, part, cols), BF),
            sds((chunks, part, cols), BF),
        ),
        grid_spec=pltpu.PrefetchScalarGridSpec(
            num_scalar_prefetch=1,
            grid=(steps,),
            in_specs=[
                whole(rows, width),
                whole(rows, width),
                whole(1, width),
                whole(rows, width),
                pl.BlockSpec((width, tile), lambda s, *_: (0, s)),
                pl.BlockSpec((tile, width), lambda s, *_: (s, 0)),
            ],
            out_specs=(
                whole(rows, width),
                whole(rows, width),
                whole(1, width),
                whole(chunks, part, cols),
                whole(chunks, part, cols),
            ),
            scratch_shapes=[pltpu.VMEM((rows, width), F32), pltpu.VMEM((rows, width), F32)],
        ),
        compiler_params=pltpu.CompilerParams(vmem_limit_bytes=56 * MIB),
        cost_estimate=pl.CostEstimate(flops=15 * 10**9, bytes_accessed=25 * 10**6, transcendentals=0),
    )(place, a3, h2, gain_ff.reshape(1, width), gy, w_ff_in, w_ff_out)


def cross_backward(dh2, o2, inv, cq, kv, e, w_cross_out):
    rows, width = cq.shape
    pairs = width // 128
    tokens = kv.shape[0]
    block_rows = query_block(rows, tokens)
    blocks = rows // block_rows

    def body(
        dh2_ref, wco_ref, o2_ref, inv_ref, cq_ref, k_ref, v_ref, e_ref,
        dcq_ref, dkt_ref, dvt_ref,
        do2,
    ):
        pair = pl.program_id(0)

        @pl.when(pair == 0)
        def _():
            do2v = dot_nt(dh2_ref[...].astype(BF), wco_ref[...]).astype(BF)
            for i in range(pairs):
                do2[i] = do2v[:, i * 128 : (i + 1) * 128]

        q0, q1 = half_masks(block_rows)
        k0, k1 = half_masks(tokens)
        qmask, kmask = (q0, q1), (k0, k1)
        lane = lax.broadcasted_iota(jnp.int32, (block_rows, 128), 1)
        low = lane < 64
        first = lax.rem(lane, 64) == 0
        second = lax.rem(lane, 64) == 1
        k, v = k_ref[...], v_ref[...]
        sums = [0.0] * 4
        for block in range(blocks):
            at = slice(block * block_rows, (block + 1) * block_rows)
            q = cq_ref[at, :]
            dof = do2[pair, at, :].astype(F32) * inv_ref[at, :]
            dob = dof.astype(BF)
            prod = dof * o2_ref[at, :].astype(F32)
            qt = jnp.transpose(q)
            dot_t = jnp.transpose(dob)
            dqs = []
            for h in range(2):
                own = low if h == 0 else jnp.logical_not(low)
                delta = -jnp.sum(jnp.where(own, prod, 0.0), -1, keepdims=True)
                hi = delta.astype(BF).astype(F32)
                feat = jnp.where(first, hi, jnp.where(second, delta - hi, 0.0)).astype(BF)
                doa = dob * qmask[h] + feat * qmask[1 - h]
                dp = dot_nt(doa, v * kmask[h] + kmask[1 - h])
                ev = e_ref[h, at, :]
                ds = (ev.astype(F32) * dp).astype(BF)
                dqs.append(dot_nn(ds, k))
                sums[h] = sums[h] + dot_nn(qt[h * 64 : (h + 1) * 64, :], ds)
                sums[2 + h] = sums[2 + h] + dot_nn(dot_t[h * 64 : (h + 1) * 64, :], ev)
            dcq_ref[at, :] = jnp.where(low, dqs[0], dqs[1]).astype(BF)
        for h in range(2):
            dkt_ref[h * 64 : (h + 1) * 64, :] = sums[h].astype(BF)
            dvt_ref[h * 64 : (h + 1) * 64, :] = sums[2 + h].astype(BF)

    sds = jax.ShapeDtypeStruct
    column = lambda n: pl.BlockSpec((n, 128), lambda p: (0, p))
    return pl.pallas_call(
        body,
        out_shape=(sds((rows, width), BF), sds((width, tokens), BF), sds((width, tokens), BF)),
        grid=(pairs,),
        in_specs=[
            pl.BlockSpec((rows, width), lambda p: (0, 0)),
            pl.BlockSpec((width, width), lambda p: (0, 0)),
            column(rows),
            column(rows),
            column(rows),
            column(tokens),
            pl.BlockSpec((tokens, 128), lambda p: (0, p + pairs)),
            pl.BlockSpec((2, rows, tokens), lambda p: (p, 0, 0)),
        ],
        out_specs=(
            column(rows),
            pl.BlockSpec((128, tokens), lambda p: (p, 0)),
            pl.BlockSpec((128, tokens), lambda p: (p, 0)),
        ),
        scratch_shapes=[pltpu.VMEM((pairs, rows, 128), BF)],
        compiler_params=pltpu.CompilerParams(vmem_limit_bytes=56 * MIB),
        cost_estimate=pl.CostEstimate(flops=15 * 10**9, bytes_accessed=25 * 10**6, transcendentals=0),
    )(dh2, w_cross_out, o2, inv, cq, kv, kv, e)


def cross_weights(
    place, dh2, o2, dcq, dkt, dvt, gathered, shard_rows, a2, h1, gain_cross,
    w_cross_kv, w_cross_q, bits, chunks,
):
    rows, width = dcq.shape
    pieces, piece_rows, _ = gathered.shape
    part = width // chunks
    half = width // 2
    cols = 2 * width
    tokens = pieces * shard_rows
    tile_pieces = min(pieces, max(1, 1024 // shard_rows))
    tile = tile_pieces * shard_rows
    steps = tokens // tile

    def body(
        place_ref, dh2_ref, o2_ref, dcq_ref, dkt_ref, dvt_ref, enc_ref, a2_ref, h1_ref,
        gc_ref, wkv_ref, wcq_ref,
        dh1_ref, gain_ref, genc_ref, keep_ref, send_ref,
        *accs,
    ):
        core, blk = place_ref[0], place_ref[1]
        step = pl.program_id(0)

        @pl.when(step == 0)
        def _():
            dcqv = dcq_ref[...]
            da2 = dot_nt(dcqv, wcq_ref[...])
            dv, dgain = rms_back(da2, h1_ref[...], gc_ref[...])
            dh1_ref[...] = dh2_ref[...] + dv
            gain_ref[...] = dgain
            for which, ref in ((core, keep_ref), (1 - core, send_ref)):
                at = pl.ds(pl.multiple_of(which * half, 128), half)
                gco = dot_tn(o2_ref[...], dh2_ref[:, at].astype(BF))
                store_chunks(ref, gco, 0, blk, bits, chunks)
                gcq = dot_tn(a2_ref[...], dcq_ref[:, at])
                store_chunks(ref, gcq, half, blk, bits, chunks)

        wkv = wkv_ref[...]
        genc = dot_tn(dkt_ref[...], jnp.transpose(wkv[:, :width]))
        genc = genc + dot_tn(dvt_ref[...], jnp.transpose(wkv[:, width:]))
        genc_ref[...] = genc.astype(BF)
        enct = jnp.concatenate(
            [jnp.transpose(enc_ref[i, :shard_rows, :]) for i in range(tile_pieces)], 1
        )
        gk = dot_nt(enct, dkt_ref[...])
        gv = dot_nt(enct, dvt_ref[...])
        if accs:
            gk = gk + jnp.where(step == 0, 0.0, accs[0][...])
            gv = gv + jnp.where(step == 0, 0.0, accs[1][...])
            accs[0][...] = gk
            accs[1][...] = gv

        @pl.when(step == steps - 1)
        def _():
            for core_is in range(2):
                own, other = (gk, gv) if core_is == 0 else (gv, gk)

                @pl.when(core == core_is)
                def _():
                    store_chunks(keep_ref, own, width, blk, bits, chunks)
                    store_chunks(send_ref, other, width, blk, bits, chunks)

    sds = jax.ShapeDtypeStruct
    whole = lambda *shape: pl.BlockSpec(shape, lambda s, *_: (0,) * len(shape))
    return pl.pallas_call(
        body,
        out_shape=(
            sds((rows, width), F32),
            sds((1, width), F32),
            sds((tokens, width), BF),
            sds((chunks, part, cols), BF),
            sds((chunks, part, cols), BF),
        ),
        grid_spec=pltpu.PrefetchScalarGridSpec(
            num_scalar_prefetch=1,
            grid=(steps,),
            in_specs=[
                whole(rows, width),
                whole(rows, width),
                whole(rows, width),
                pl.BlockSpec((width, tile), lambda s, *_: (0, s)),
                pl.BlockSpec((width, tile), lambda s, *_: (0, s)),
                pl.BlockSpec((tile_pieces, piece_rows, width), lambda s, *_: (s, 0, 0)),
                whole(rows, width),
                whole(rows, width),
                whole(1, width),
                whole(width, 2 * width),
                whole(width, width),
            ],
            out_specs=(
                whole(rows, width),
                whole(1, width),
                pl.BlockSpec((tile, width), lambda s, *_: (s, 0)),
                whole(chunks, part, cols),
                whole(chunks, part, cols),
            ),
            scratch_shapes=[pltpu.VMEM((width, width), F32)] * (2 if steps > 1 else 0),
        ),
        compiler_params=pltpu.CompilerParams(vmem_limit_bytes=56 * MIB),
        cost_estimate=pl.CostEstimate(flops=10 * 10**9, bytes_accessed=25 * 10**6, transcendentals=0),
    )(
        place, dh2, o2, dcq, dkt, dvt, gathered, a2, h1, gain_cross.reshape(1, width),
        w_cross_kv, w_cross_q,
    )


def self_backward(
    place, dh1, o1, qkv, p1, a1, x, gain_self, w_self_out, w_qkv, gain_cross_grad, gain_ff_grad,
    bucket_count, heads, bits, chunks,
):
    rows, width = x.shape
    pairs = heads // 2
    groups = rows // GROUP
    ids = bucket_ids(bucket_count)
    used = sorted(set(ids[ids >= 0].tolist()))
    part = width // chunks
    half = width // 2
    cols = half + 3 * half
    ids_small = np.concatenate([ids[t * TLEN : (t + 1) * TLEN] for t in range(1)], 0)
    ids_small = np.tile(ids_small[:, :TLEN], (1, GROUP // TLEN))

    def body(
        place_ref, dh1_ref, o1_ref, qkv_ref, p1_ref, a1_ref, x_ref, gs_ref, wso_ref, wqkv_ref,
        ids_ref, ggc_ref, ggf_ref,
        out_ref, keep_ref, send_ref, misc_ref,
        do1, dqkv, acc,
    ):
        core, blk = place_ref[0], place_ref[1]
        gs = dh1_ref[...].astype(BF)
        do1[...] = dot_nt(gs, wso_ref[...]).astype(BF)
        m0, m1 = half_masks(GROUP)
        acc[...] = jnp.zeros_like(acc)

        def attend(g, carry):
            at = pl.ds(pl.multiple_of(g * GROUP, GROUP), GROUP)
            for pair in range(pairs):
                lo = pair * 128
                q = qkv_ref[at, lo : lo + 128]
                k = qkv_ref[at, width + lo : width + lo + 128]
                v = qkv_ref[at, 2 * width + lo : 2 * width + lo + 128]
                do = do1[at, lo : lo + 128]
                do_two = jnp.concatenate([do * m0, do * m1], 0)
                pb = p1_ref[g, pair]
                pf = pb.astype(F32)
                dp = dot_nt(do_two, v)
                ds = (pf * (dp - jnp.sum(pf * dp, -1, keepdims=True))).astype(BF)
                dsf = ds.astype(F32)
                for h in range(2):
                    total = dsf[h * GROUP : h * GROUP + TLEN]
                    for t in range(1, GROUP // TLEN):
                        total = total + dsf[h * GROUP + t * TLEN : h * GROUP + (t + 1) * TLEN]
                    acc[2 * pair + h] += total
                dq = dot_nn(
                    jnp.concatenate([ds[:GROUP], ds[GROUP:]], 1),
                    jnp.concatenate([k * m0, k * m1], 0),
                )
                dk = dot_tn(ds, jnp.concatenate([q * m0, q * m1], 0))
                dv = dot_tn(pb, do_two)
                dqkv[at, lo : lo + 128] = dq.astype(BF)
                dqkv[at, width + lo : width + lo + 128] = dk.astype(BF)
                dqkv[at, 2 * width + lo : 2 * width + lo + 128] = dv.astype(BF)
            return carry

        lax.fori_loop(0, groups, attend, 0)
        for which, ref in ((1 - core, send_ref), (core, keep_ref)):
            gso = dot_tn(o1_ref[...], dh1_ref[:, pl.ds(pl.multiple_of(which * half, 128), half)].astype(BF))
            store_chunks(ref, gso, 0, blk, bits, chunks)
            gqkv = dot_tn(a1_ref[...], dqkv[:, pl.ds(pl.multiple_of(which * 3 * half, 128), 3 * half)])
            store_chunks(ref, gqkv, half, blk, bits, chunks)
        da1 = dot_nt(dqkv[...], wqkv_ref[...])
        dvx, dgain = rms_back(da1, x_ref[...].astype(F32), gs_ref[...])
        out_ref[...] = dh1_ref[...] + dvx
        idv = ids_ref[...]
        lane = lax.broadcasted_iota(jnp.int32, (16, 128), 1)
        bias = jnp.zeros((16, 128), F32)
        accv = acc[...]
        pad = jnp.zeros((16 - heads, 1), F32)
        for b in used:
            part_sum = jnp.sum(jnp.where((idv == b)[None], accv, 0.0), axis=1)
            col = jnp.sum(part_sum, -1, keepdims=True)
            bias = jnp.where(lane == b, jnp.concatenate([col, pad], 0), bias)
        misc_ref[...] = jnp.zeros_like(misc_ref)
        misc_ref[0:16, 0:128] = bias
        misc_ref[12:13, 0:width] = dgain
        misc_ref[13:14, 0:width] = ggc_ref[...]
        misc_ref[14:15, 0:width] = ggf_ref[...]

    sds = jax.ShapeDtypeStruct
    return call(
        body,
        (
            sds((rows, width), F32),
            sds((chunks, part, cols), BF),
            sds((chunks, part, cols), BF),
            sds((16, cols), F32),
        ),
        [SMEM] + [VMEM] * 12,
        (VMEM,) * 4,
        [
            pltpu.VMEM((rows, width), BF),
            pltpu.VMEM((rows, 3 * width), BF),
            pltpu.VMEM((heads, TLEN, GROUP), F32),
        ],
        flops=14 * 10**9,
        nbytes=25 * 10**6,
    )(
        place, dh1, o1, qkv, p1, a1, x, gain_self.reshape(1, width), w_self_out, w_qkv,
        jnp.asarray(ids_small), gain_cross_grad, gain_ff_grad,
    )


def swap(value, axis, bit):
    size = lax.axis_size(axis)
    return lax.ppermute(value, axis, [(i, i ^ bit) for i in range(size)])


def add_up(terms):
    total = terms[0].astype(F32)
    for term in terms[1:]:
        total = total + term.astype(F32)
    return total


def reduce_chunks(keep, send, bits, dp_bits, extra=None):
    chunks, part, cols = keep.shape
    rows = chunks * part
    terms = [keep.reshape(rows, cols)]
    send = send.reshape(rows, cols)
    if extra is not None:
        extra_low = extra.astype(BF)
        got = swap(jnp.concatenate([send, extra_low], 0), "dp", 1)
        terms.append(got[:rows])
        extra = extra_low.astype(F32) + got[rows:].astype(F32)
    else:
        terms.append(swap(send, "dp", 1))
    for bit in bits:
        rows //= 2
        out = add_up([t[rows : 2 * rows] for t in terms]).astype(BF)
        terms = [t[:rows] for t in terms]
        if extra is not None:
            extra_low = extra.astype(BF)
            got = swap(jnp.concatenate([out, extra_low], 0), "blk", bit)
            extra = extra_low.astype(F32) + got[rows:].astype(F32)
            terms.append(got[:rows])
        else:
            terms.append(swap(out, "blk", bit))
    total = add_up(terms)
    for bit in dp_bits:
        if bit == 1:
            continue
        out = total.astype(BF)
        if extra is not None:
            extra_low = extra.astype(BF)
            got = swap(jnp.concatenate([out, extra_low], 0), "dp", bit)
            extra = extra_low.astype(F32) + got[rows:].astype(F32)
            total = out.astype(F32) + got[:rows].astype(F32)
        else:
            total = out.astype(F32) + swap(out, "dp", bit).astype(F32)
    own = total.astype(BF)
    return own, swap(own, "dp", 1), extra


def join_halves(place, own, other, widths, stacks):
    part = own.shape[0]

    def body(place_ref, own_ref, other_ref, *outs):
        core = place_ref[0]
        col = 0
        for out, width, stack in zip(outs, widths, stacks):
            half = width // 2
            for j in range(stack):
                for which, ref in ((core, own_ref), (1 - core, other_ref)):
                    at = pl.ds(pl.multiple_of(which * half, 128), half)
                    out[j * part : (j + 1) * part, at] = ref[:, col : col + half].astype(F32)
                col += half

    return call(
        body,
        tuple(jax.ShapeDtypeStruct((stack * part, width), F32) for width, stack in zip(widths, stacks)),
        [SMEM, VMEM, VMEM],
        (VMEM,) * len(widths),
        limit=24,
        nbytes=4 * 10**6,
    )(place, own, other)


def local(
    dec_in,
    encodings,
    enc_question,
    enc_valid,
    tgt_question,
    gain_self,
    w_qkv,
    rel_bias,
    w_self_out,
    gain_cross,
    w_cross_q,
    w_cross_kv,
    w_cross_out,
    gain_ff,
    w_ff_in,
    w_ff_out,
    grad_out,
):
    x = dec_in[0]
    gy = grad_out[0]
    rows, width = x.shape
    bucket_count, heads = rel_bias.shape
    hidden = w_ff_in.shape[1]
    chunks = lax.axis_size("blk")
    dp_size = lax.axis_size("dp")
    shard_rows = encodings.shape[1]
    bits = [1 << i for i in range(chunks.bit_length() - 1)]
    dp_bits = [1 << i for i in range(dp_size.bit_length() - 1)]
    blk = lax.axis_index("blk")
    core = lax.rem(lax.axis_index("dp"), 2)
    place = jnp.stack([core, blk]).astype(jnp.int32)

    tags = jnp.where(enc_valid[0] == 1, enc_question[0], -1).astype(BF)
    tag_rows = jnp.zeros((16, width), BF).at[0, :shard_rows].set(tags)
    gathered = jnp.concatenate([encodings[0], tag_rows], 0)[None]
    for bit in reversed(bits):
        gathered = jnp.concatenate([gathered, swap(gathered, "blk", bit)], 0)

    a1, qkv, p1, o1, h1, a2, cq = self_forward(
        x, gain_self, w_qkv, rel_bias, w_self_out, gain_cross, w_cross_q
    )
    kv, e, inv, o2, h2, a3 = cross_forward(
        gathered, shard_rows, tgt_question[0], cq, h1, w_cross_kv, w_cross_out, gain_ff
    )
    out, dh2, gain_ff_grad, keep_ff, send_ff = feed_forward(
        place, a3, h2, gain_ff, gy, w_ff_in, w_ff_out, bits, chunks
    )
    own_ff, other_ff, _ = reduce_chunks(keep_ff, send_ff, bits, dp_bits)
    dcq, dkt, dvt = cross_backward(dh2, o2, inv, cq, kv, e, w_cross_out)
    dh1, gain_cross_grad, genc, keep_x, send_x = cross_weights(
        place, dh2, o2, dcq, dkt, dvt, gathered, shard_rows, a2, h1, gain_cross,
        w_cross_kv, w_cross_q, bits, chunks,
    )
    own_x, other_x, _ = reduce_chunks(keep_x, send_x, bits, dp_bits)
    terms = [genc]
    left = chunks * shard_rows
    for bit in bits:
        left //= 2
        sent = add_up([t[left : 2 * left] for t in terms]).astype(BF)
        terms = [t[:left] for t in terms] + [swap(sent, "blk", bit)]
    grad_enc = add_up(terms)
    grad_dec, keep_s, send_s, misc = self_backward(
        place, dh1, o1, qkv, p1, a1, x, gain_self, w_self_out, w_qkv, gain_cross_grad, gain_ff_grad,
        bucket_count, heads, bits, chunks,
    )
    own_s, other_s, misc = reduce_chunks(keep_s, send_s, bits, dp_bits, misc)
    misc = misc.astype(BF).astype(F32)

    grad_ff_in, grad_ff_out = join_halves(
        place, own_ff, other_ff, (hidden, width), (1, hidden // width)
    )
    grad_cross_out, grad_cross_q, grad_cross_kv = join_halves(
        place, own_x, other_x, (width, width, 2 * width), (1, 1, 1)
    )
    grad_self_out, grad_qkv = join_halves(place, own_s, other_s, (width, 3 * width), (1, 1))
    part = width // chunks
    gains = lax.dynamic_slice(misc, (12, blk * part), (3, part))
    bias_part = bucket_count // chunks
    grad_bias = lax.dynamic_slice(misc, (0, blk * bias_part), (heads, bias_part)).T
    return (
        out[None],
        grad_dec[None],
        grad_enc[None],
        gains[0],
        grad_qkv,
        grad_bias,
        grad_self_out,
        gains[1],
        grad_cross_q,
        grad_cross_kv,
        grad_cross_out,
        gains[2],
        grad_ff_in,
        grad_ff_out,
    )


def solution(mesh):
    return jax.shard_map(
        local,
        mesh=mesh,
        in_specs=(
            P("dp", "blk", None),
            P("dp", "blk", None),
            P("dp", "blk"),
            P("dp", "blk"),
            P("dp", "blk"),
            P(),
            P(),
            P(),
            P(),
            P(),
            P(),
            P(),
            P(),
            P(),
            P(),
            P(),
            P("dp", "blk", None),
        ),
        out_specs=(
            P("dp", "blk", None),
            P("dp", "blk", None),
            P("dp", "blk", None),
            P("blk"),
            P("blk", None),
            P("blk", None),
            P("blk", None),
            P("blk"),
            P("blk", None),
            P("blk", None),
            P("blk", None),
            P("blk"),
            P("blk", None),
            P("blk", None),
        ),
        check_vma=False,
    )
```

time: 924 us -> 379 us (0.41)
  waiting for transfers between devices: 528 us -> 160 us
  matrix products: 159 us -> 0 us
  Pallas kernels: 0 us -> 124 us
  local copies, waits for them, and re-layouts: 96.5 us -> 13 us
  blocking collectives: 60.3 us -> 0 us
  starting transfers between devices: 1.05 us -> 46.3 us
  other arithmetic: 49.8 us -> 30.1 us
  between operations: 16.5 us -> 1.35 us
    reduce_scatter x6 -> x0, waiting for transfers between devices: 403 us -> none  [the longest x1 98.8 us: local(): lax.psum_scatter(grad_w_two.astype(jnp.bfloat16), 'blk', scatter_dimensio...]
    ppermute x0 -> x24, waiting for transfers between devices: none -> 160 us  [swap(): return lax.ppermute(value, axis, [(i, i ^ bit) for i in range(size)])]
    dot_general x43 -> x0, matrix products: 159 us -> none  [the longest x2 14.5 us: block_grads(): jnp.einsum('qhd,khd->hqk', grad_cross_att, kv_heads[:, 1], preferred_elem...]
    pallas_call x0 -> x9, Pallas kernels: none -> 124 us  [the longest x1 27.9 us: feed_forward(): pl.pallas_call(body, out_shape=(sds((rows, width), BF), sds((rows, width)...]
    unnamed x12 -> x0, waiting for transfers between devices: 74.9 us -> none
    psum x1 -> x0, waiting for transfers between devices: 50.1 us -> none  [local(): lax.psum(shares[6].astype(jnp.bfloat16), 'dp').astype(jnp.float32)]
    ppermute x0 -> x24, starting transfers between devices: none -> 46.3 us  [swap(): return lax.ppermute(value, axis, [(i, i ^ bit) for i in range(size)])]
    unnamed x123 -> x16, local copies, waits for them, and re-layouts: 33.6 us -> 2.74 us
  transfers between devices with their start and end apart: 10 -> 24, of which waited for: 7 -> 13; matrix products, arithmetic and copies ran while one was open for 16% -> 10% of each run, Pallas kernels for 0% -> 10%
where the time goes in v1:
time: 379 us; the launch traced here: 374 us
  waiting for transfers between devices  160 us (42%)
  Pallas kernels  124 us (33%)
  starting transfers between devices  46.3 us (12%)
  other arithmetic  30.1 us (8%)
  local copies, waits for them, and re-layouts  13 us (3%)
    ppermute x24, waiting for transfers between devices, swap(): return lax.ppermute(value, axis, [(i, i ^ bit) for i in range(size)])  160 us
    ppermute x24, starting transfers between devices, swap(): return lax.ppermute(value, axis, [(i, i ^ bit) for i in range(size)])  46.3 us
    pallas_call x1, Pallas kernels, feed_forward(): pl.pallas_call(body, out_shape=(sds((rows, width), BF), sds((rows, width)...  27.9 us
    pallas_call x1, Pallas kernels, cross_forward(): call(body, (sds((tokens, 2 * width), BF), sds((2 * pairs, rows, tokens),...  22.2 us
    pallas_call x1, Pallas kernels, self_backward(): call(body, (sds((rows, width), F32), sds((chunks, part, cols), BF), sds((...  20.5 us
    pallas_call x1, Pallas kernels, cross_backward(): pl.pallas_call(body, out_shape=(sds((rows, width), BF), sds((width, token...  17.3 us
    pallas_call x1, Pallas kernels, cross_weights(): pl.pallas_call(body, out_shape=(sds((rows, width), F32), sds((1, width),...  17 us
    pallas_call x1, Pallas kernels, self_forward(): call(body, (sds((rows, width), BF), sds((rows, 3 * width), BF), sds((grou...  13.5 us
  transfers between devices with their start and end apart: 24, of which 13 were waited for; matrix products, arithmetic and copies ran while one was open for 10% of the time, Pallas kernels for 10%

profile of v1, /device:TPU:1, one launch (start us, length us, event | category | flops | bytes accessed | tf_op | source)
XLA Modules:
  0.0 374.1 jit_solution(11330410492927219887)
XLA Ops:
  2.3 3.2 collective-permute-start
  5.5 9.9 %collective-permute-done = bf16[1,144,768]{2,1,0:T(8,128)(2,1)S(1)} collective-permute-done((bf16[1,144,768]{2,1,0:T(8,128)(2,1)S(1)}, bf16[1,144,768]{2,1,0:T(8,128)(2,1)S(1)}, u32[]{:S(2)}, u32[]{:S(2)}) %collective-permute-start) | collective-permute-done | bytes 221216 | tf_op jit(solution)/shard_map/ppermute | solution.py:684
  22.4 3.5 collective-permute-done.1
  27.1 13.5 %shard_map.290 = (bf16[512,768]{1,0:T(8,128)(2,1)}, bf16[512,2304]{1,0:T(8,128)(2,1)}, bf16[4,6,256,128]{3,2,1,0:T(8,128)(2,1)}, bf16[512,768]{1,0:T(8,128)(2,1)...) custom-call(bf16[512,768]{1,0:T(8,128)(2,1)} %bitcast.64, f32[1,768]{1,0:T(1,128)} %reshape.122.gs_ref, ...), custom_call_target="tpu_custom_call" | custom-call | flops 12000000000 | bytes 16000000 | tf_op jit(solution)/shard_map/pallas_call | solution.py:159
  40.6 4.5 %collective-permute-done.2 = bf16[4,144,768]{2,1,0:T(8,128)(2,1)S(1)} collective-permute-done((bf16[4,144,768]{2,1,0:T(8,128)(2,1)S(1)}, bf16[4,144,768]{2,1,0:T(8,128)(2,1)S(1)}, u32[]{:S(2)}, u32[]{:S(2)}) %collective-permute-start.2) | collective-permute-done | bytes 884768 | tf_op jit(solution)/shard_map/ppermute | solution.py:684
  46.5 22.2 %shard_map.291 = (bf16[1024,1536]{1,0:T(8,128)(2,1)}, bf16[12,512,1024]{2,1,0:T(8,128)(2,1)}, f32[512,768]{1,0:T(8,128)}, bf16[512,768]{1,0:T(8,128)(2,1)}, f32[...) custom-call(bf16[8,144,768]{2,1,0:T(8,128)(2,1)} %pad_maximum_fusion.1.enc_ref, s32[16]{0:T(128)} %bitcast.66, ...), custom_call_target="tpu_custom_call" | custom-call | flops 16000000000 | bytes 30000000 | tf_op jit(solution)/shard_map/pallas_call | solution.py:257
  68.7 27.9 %shard_map.292 = (bf16[512,768]{1,0:T(8,128)(2,1)}, f32[512,768]{1,0:T(8,128)}, f32[1,768]{1,0:T(1,128)}, bf16[8,96,3072]{2,1,0:T(8,128)(2,1)}, bf16[8,96,3072]{2,1,0:T(8,128)(2,1)}) custom-call(s32[2]{0:T(128)} %pad_add_fusion.place_ref, bf16[512,768]{1,0:T(8,128)(2,1)} %get-tuple-element.65.a3_ref, f32[512,768]{1,0:T(8,128)} %get-tuple-element.66.h2_ref, ...), custom_call_target="tpu_custom_call" | custom-call | flops 15000000512 | bytes 25000000 | tf_op jit(solution)/shard_map/pallas_call | solution.py:355
  96.6 17.3 %shard_map.293 = (bf16[512,768]{1,0:T(8,128)(2,1)}, bf16[768,1024]{1,0:T(8,128)(2,1)}, bf16[768,1024]{1,0:T(8,128)(2,1)}) custom-call(f32[512,768]{1,0:T(8,128)} %get-tuple-element.68.dh2_ref, bf16[768,768]{1,0:T(8,128)(2,1)} %wco_ref.3, bf16[512,768]{1,0:T(8,128)(2,1)} %get-tuple-element.69.o2_ref, f32[512,768]{1,0:T(8,128)} %get-tuple-element.70.inv_ref, ...), custom_call_target="tpu_custom_call" | custom-call | flops 15000000512 | bytes 25000000 | tf_op jit(solution)/shard_map/pallas_call | solution.py:446
  113.9 17.0 %shard_map.294 = (f32[512,768]{1,0:T(8,128)}, f32[1,768]{1,0:T(1,128)}, bf16[1024,768]{1,0:T(8,128)(2,1)}, bf16[8,96,1536]{2,1,0:T(8,128)(2,1)}, bf16[8,96,1536]{2,1,0:T(8,128)(2,1)}) custom-call(s32[2]{0:T(128)} %pad_add_fusion.place_ref, f32[512,768]{1,0:T(8,128)} %get-tuple-element.68.dh2_ref, bf16[512,768]{1,0:T(8,128)(2,1)} %get-tuple-element.69.o2_ref, ...), custom_call_target="tpu_custom_call" | custom-call | flops 10000000000 | bytes 25000000 | tf_op jit(solution)/shard_map/pallas_call | solution.py:535
  134.0 20.5 %shard_map.295 = (f32[512,768]{1,0:T(8,128)}, bf16[8,96,1536]{2,1,0:T(8,128)(2,1)}, bf16[8,96,1536]{2,1,0:T(8,128)(2,1)}, f32[16,1536]{1,0:T(8,128)}) custom-call(s32[2]{0:T(128)} %pad_add_fusion.place_ref, f32[512,768]{1,0:T(8,128)} %get-tuple-element.77.dh1_ref, bf16[512,768]{1,0:T(8,128)(2,1)} %get-tuple-element.78.o1_ref, ...), custom_call_target="tpu_custom_call" | custom-call | flops 14000000000 | bytes 25000000 | tf_op jit(solution)/shard_map/pallas_call | solution.py:659
  167.3 10.0 %collective-permute-done.3 = bf16[512,768]{1,0:T(8,128)(2,1)S(1)} collective-permute-done((bf16[512,768]{1,0:T(8,128)(2,1)S(1)}, bf16[512,768]{1,0:T(8,128)(2,1)S(1)}, u32[]{:S(2)}, u32[]{:S(2)}) %collective-permute-start.3) | collective-permute-done | bytes 786464 | tf_op jit(solution)/shard_map/ppermute | solution.py:684
  189.7 3.2 collective-permute-start.5
  192.9 9.8 %collective-permute-done.13 = bf16[384,1536]{1,0:T(8,128)(2,1)} collective-permute-done((bf16[384,1536]{1,0:T(8,128)(2,1)}, bf16[384,1536]{1,0:T(8,128)(2,1)}, u32[]{:S(2)}, u32[]{:S(2)}) %collective-permute-start.13) | collective-permute-done | bytes 1179680 | tf_op jit(solution)/shard_map/ppermute | solution.py:684
  206.0 23.0 %collective-permute-done.7 = bf16[400,1536]{1,0:T(8,128)(2,1)} collective-permute-done((bf16[400,1536]{1,0:T(8,128)(2,1)}, bf16[400,1536]{1,0:T(8,128)(2,1)}, u32[]{:S(2)}, u32[]{:S(2)}) %collective-permute-start.7) | collective-permute-done | bytes 1228832 | tf_op jit(solution)/shard_map/ppermute | solution.py:684
  240.1 3.2 collective-permute-start.15
  243.3 13.7 %collective-permute-done.8 = bf16[208,1536]{1,0:T(8,128)(2,1)S(1)} collective-permute-done((bf16[208,1536]{1,0:T(8,128)(2,1)S(1)}, bf16[208,1536]{1,0:T(8,128)(2,1)S(1)}, u32[]{:S(2)}, u32[]{:S(2)}) %collective-permute-start.8) | collective-permute-done | bytes 639008 | tf_op jit(solution)/shard_map/ppermute | solution.py:684
  258.2 26.6 %collective-permute-done.19 = bf16[384,3072]{1,0:T(8,128)(2,1)S(1)} collective-permute-done((bf16[384,3072]{1,0:T(8,128)(2,1)S(1)}, bf16[384,3072]{1,0:T(8,128)(2,1)S(1)}, u32[]{:S(2)}, u32[]{:S(2)}) %collective-permute-start.19) | collective-permute-done | bytes 2359328 | tf_op jit(solution)/shard_map/ppermute | solution.py:684
  288.8 3.2 collective-permute-start.9
  294.5 25.1 %collective-permute-done.9 = bf16[112,1536]{1,0:T(8,128)(2,1)S(1)} collective-permute-done((bf16[112,1536]{1,0:T(8,128)(2,1)S(1)}, bf16[112,1536]{1,0:T(8,128)(2,1)S(1)}, u32[]{:S(2)}, u32[]{:S(2)}) %collective-permute-start.9) | collective-permute-done | bytes 344096 | tf_op jit(solution)/shard_map/ppermute | solution.py:684
  322.5 3.2 collective-permute-start.21
  327.0 22.3 %collective-permute-done.21 = bf16[96,3072]{1,0:T(8,128)(2,1)S(1)} collective-permute-done((bf16[96,3072]{1,0:T(8,128)(2,1)S(1)}, bf16[96,3072]{1,0:T(8,128)(2,1)S(1)}, u32[]{:S(2)}, u32[]{:S(2)}) %collective-permute-start.21) | collective-permute-done | bytes 589856 | tf_op jit(solution)/shard_map/ppermute | solution.py:684
  352.4 3.7 collective-permute-start.17
  356.2 6.4 %collective-permute-done.22 = bf16[96,3072]{1,0:T(8,128)(2,1)S(1)} collective-permute-done((bf16[96,3072]{1,0:T(8,128)(2,1)S(1)}, bf16[96,3072]{1,0:T(8,128)(2,1)S(1)}, u32[]{:S(2)}, u32[]{:S(2)}) %collective-permute-start.22) | collective-permute-done | bytes 589856 | tf_op jit(solution)/shard_map/ppermute | solution.py:684
  362.7 4.3 %collective-permute-start.23 = (bf16[96,3072]{1,0:T(8,128)(2,1)S(1)}, bf16[96,3072]{1,0:T(8,128)(2,1)S(1)}, u32[]{:S(2)}, u32[]{:S(2)}) collective-permute-start(bf16[96,3072]{1,0:T(8,128)(2,1)S(1)} %add_convert_fusion.own_ref), channel_id=1, source_target_pairs={{0,8},{8,0},{16,24},{24,16},{1,9},{9,1},{17,25},{25,17},{2,10},{10... | collective-permute-start | bytes 1769480 | tf_op jit(solution)/shard_map/ppermute | solution.py:684
  (97 shorter events, 75.7 us)
Async XLA Ops:
  2.3 13.1 %collective-permute-start = (bf16[1,144,768]{2,1,0:T(8,128)(2,1)S(1)}, bf16[1,144,768]{2,1,0:T(8,128)(2,1)S(1)}, u32[]{:S(2)}, u32[]{:S(2)}) collective-permute-start(bf16[1,144,768]{2,1,0:T(8,128)(2,1)S(1)} %fusion.32), channel_id=1, source_target_pairs={{0,4},{1,5},{2,6},{3,7},{4,0},{5,1},{6,2},{7,3},{8,12},{9,13},{10,... | collective-permute-start | bytes 663560 | tf_op jit(solution)/shard_map/ppermute | solution.py:684
  15.4 10.5 %collective-permute-start.1 = (bf16[2,144,768]{2,1,0:T(8,128)(2,1)S(1)}, bf16[2,144,768]{2,1,0:T(8,128)(2,1)S(1)}, u32[]{:S(2)}, u32[]{:S(2)}) collective-permute-start(bf16[2,144,768]{2,1,0:T(8,128)(2,1)S(1)} %pad_maximum_fusion.5), channel_id=1, source_target_pairs={{0,2},{1,3},{2,0},{3,1},{4,6},{5,7},{6,4},{7,5},{8,10},{9,11},{10,... | collective-permute-start | bytes 1327112 | tf_op jit(solution)/shard_map/ppermute | solution.py:684
  26.0 19.1 %collective-permute-start.2 = (bf16[4,144,768]{2,1,0:T(8,128)(2,1)S(1)}, bf16[4,144,768]{2,1,0:T(8,128)(2,1)S(1)}, u32[]{:S(2)}, u32[]{:S(2)}) collective-permute-start(bf16[4,144,768]{2,1,0:T(8,128)(2,1)S(1)} %pad_maximum_fusion.3), channel_id=1, source_target_pairs={{0,1},{1,0},{2,3},{3,2},{4,5},{5,4},{6,7},{7,6},{8,9},{9,8},{10,11... | collective-permute-start | bytes 2654216 | tf_op jit(solution)/shard_map/ppermute | solution.py:684
  131.0 29.0 %collective-permute-start.12 = (bf16[768,1536]{1,0:T(8,128)(2,1)}, bf16[768,1536]{1,0:T(8,128)(2,1)S(1)}, u32[]{:S(2)}, u32[]{:S(2)}) collective-permute-start(bf16[768,1536]{1,0:T(8,128)(2,1)} %bitcast.62), channel_id=1, source_target_pairs={{0,8},{8,0},{16,24},{24,16},{1,9},{9,1},{17,25},{25,17},{2,10},{10... | collective-permute-start | bytes 7077896 | tf_op jit(solution)/shard_map/ppermute | solution.py:684
  157.4 7.3 %collective-permute-start.6 = (bf16[784,1536]{1,0:T(8,128)(2,1)S(1)}, bf16[784,1536]{1,0:T(8,128)(2,1)S(1)}, u32[]{:S(2)}, u32[]{:S(2)}) collective-permute-start(bf16[784,1536]{1,0:T(8,128)(2,1)S(1)} %pad_maximum_fusion), channel_id=1, source_target_pairs={{0,8},{8,0},{16,24},{24,16},{1,9},{9,1},{17,25},{25,17},{2,10},{10... | collective-permute-start | bytes 7225352 | tf_op jit(solution)/shard_map/ppermute | solution.py:684
  157.5 72.8 %collective-permute-start.18 = (bf16[768,3072]{1,0:T(8,128)(2,1)}, bf16[768,3072]{1,0:T(8,128)(2,1)}, u32[]{:S(2)}, u32[]{:S(2)}) collective-permute-start(bf16[768,3072]{1,0:T(8,128)(2,1)} %bitcast.61), channel_id=1, source_target_pairs={{0,8},{8,0},{16,24},{24,16},{1,9},{9,1},{17,25},{25,17},{2,10},{10... | collective-permute-start | bytes 14155784 | tf_op jit(solution)/shard_map/ppermute | solution.py:684
  158.1 19.2 %collective-permute-start.3 = (bf16[512,768]{1,0:T(8,128)(2,1)S(1)}, bf16[512,768]{1,0:T(8,128)(2,1)S(1)}, u32[]{:S(2)}, u32[]{:S(2)}) collective-permute-start(bf16[512,768]{1,0:T(8,128)(2,1)S(1)} %slice.272), channel_id=1, source_target_pairs={{0,1},{1,0},{2,3},{3,2},{4,5},{5,4},{6,7},{7,6},{8,9},{9,8},{10,11... | collective-permute-start | bytes 2359304 | tf_op jit(solution)/shard_map/ppermute | solution.py:684
  161.8 40.8 %collective-permute-start.13 = (bf16[384,1536]{1,0:T(8,128)(2,1)}, bf16[384,1536]{1,0:T(8,128)(2,1)}, u32[]{:S(2)}, u32[]{:S(2)}) collective-permute-start(bf16[384,1536]{1,0:T(8,128)(2,1)} %fusion.3), channel_id=1, source_target_pairs={{0,1},{1,0},{2,3},{3,2},{4,5},{5,4},{6,7},{7,6},{8,9},{9,8},{10,11... | collective-permute-start | bytes 3538952 | tf_op jit(solution)/shard_map/ppermute | solution.py:684
  166.3 62.7 %collective-permute-start.7 = (bf16[400,1536]{1,0:T(8,128)(2,1)}, bf16[400,1536]{1,0:T(8,128)(2,1)}, u32[]{:S(2)}, u32[]{:S(2)}) collective-permute-start(bf16[400,1536]{1,0:T(8,128)(2,1)} %pad_maximum_fusion.2), channel_id=1, source_target_pairs={{0,1},{1,0},{2,3},{3,2},{4,5},{5,4},{6,7},{7,6},{8,9},{9,8},{10,11... | collective-permute-start | bytes 3686408 | tf_op jit(solution)/shard_map/ppermute | solution.py:684
  178.1 10.4 %collective-permute-start.4 = (bf16[256,768]{1,0:T(8,128)(2,1)}, bf16[256,768]{1,0:T(8,128)(2,1)}, u32[]{:S(2)}, u32[]{:S(2)}) collective-permute-start(bf16[256,768]{1,0:T(8,128)(2,1)} %add_convert_fusion.1), channel_id=1, source_target_pairs={{0,2},{1,3},{2,0},{3,1},{4,6},{5,7},{6,4},{7,5},{8,10},{9,11},{10,... | collective-permute-start | bytes 1179656 | tf_op jit(solution)/shard_map/ppermute | solution.py:684
  189.7 47.4 %collective-permute-start.5 = (bf16[128,768]{1,0:T(8,128)(2,1)S(1)}, bf16[128,768]{1,0:T(8,128)(2,1)S(1)}, u32[]{:S(2)}, u32[]{:S(2)}) collective-permute-start(bf16[128,768]{1,0:T(8,128)(2,1)S(1)} %add_convert_fusion.4), channel_id=1, source_target_pairs={{0,4},{1,5},{2,6},{3,7},{4,0},{5,1},{6,2},{7,3},{8,12},{9,13},{10,... | collective-permute-start | bytes 589832 | tf_op jit(solution)/shard_map/ppermute | solution.py:684
  203.9 35.0 %collective-permute-start.14 = (bf16[192,1536]{1,0:T(8,128)(2,1)S(1)}, bf16[192,1536]{1,0:T(8,128)(2,1)S(1)}, u32[]{:S(2)}, u32[]{:S(2)}) collective-permute-start(bf16[192,1536]{1,0:T(8,128)(2,1)S(1)} %fusion.13), channel_id=1, source_target_pairs={{0,2},{1,3},{2,0},{3,1},{4,6},{5,7},{6,4},{7,5},{8,10},{9,11},{10,... | collective-permute-start | bytes 1769480 | tf_op jit(solution)/shard_map/ppermute | solution.py:684
  232.8 52.0 %collective-permute-start.19 = (bf16[384,3072]{1,0:T(8,128)(2,1)S(1)}, bf16[384,3072]{1,0:T(8,128)(2,1)S(1)}, u32[]{:S(2)}, u32[]{:S(2)}) collective-permute-start(bf16[384,3072]{1,0:T(8,128)(2,1)S(1)} %fusion), channel_id=1, source_target_pairs={{0,1},{1,0},{2,3},{3,2},{4,5},{5,4},{6,7},{7,6},{8,9},{9,8},{10,11... | collective-permute-start | bytes 7077896 | tf_op jit(solution)/shard_map/ppermute | solution.py:684
  234.8 22.2 %collective-permute-start.8 = (bf16[208,1536]{1,0:T(8,128)(2,1)S(1)}, bf16[208,1536]{1,0:T(8,128)(2,1)S(1)}, u32[]{:S(2)}, u32[]{:S(2)}) collective-permute-start(bf16[208,1536]{1,0:T(8,128)(2,1)S(1)} %pad_maximum_fusion.4), channel_id=1, source_target_pairs={{0,2},{1,3},{2,0},{3,1},{4,6},{5,7},{6,4},{7,5},{8,10},{9,11},{10,... | collective-permute-start | bytes 1916936 | tf_op jit(solution)/shard_map/ppermute | solution.py:684
  240.1 51.8 %collective-permute-start.15 = (bf16[96,1536]{1,0:T(8,128)(2,1)S(1)}, bf16[96,1536]{1,0:T(8,128)(2,1)S(1)}, u32[]{:S(2)}, u32[]{:S(2)}) collective-permute-start(bf16[96,1536]{1,0:T(8,128)(2,1)S(1)} %fusion.18), channel_id=1, source_target_pairs={{0,4},{1,5},{2,6},{3,7},{4,0},{5,1},{6,2},{7,3},{8,12},{9,13},{10,... | collective-permute-start | bytes 884744 | tf_op jit(solution)/shard_map/ppermute | solution.py:684
  286.7 34.2 %collective-permute-start.20 = (bf16[192,3072]{1,0:T(8,128)(2,1)S(1)}, bf16[192,3072]{1,0:T(8,128)(2,1)S(1)}, u32[]{:S(2)}, u32[]{:S(2)}) collective-permute-start(bf16[192,3072]{1,0:T(8,128)(2,1)S(1)} %fusion.2), channel_id=1, source_target_pairs={{0,2},{1,3},{2,0},{3,1},{4,6},{5,7},{6,4},{7,5},{8,10},{9,11},{10,... | collective-permute-start | bytes 3538952 | tf_op jit(solution)/shard_map/ppermute | solution.py:684
  288.8 30.9 %collective-permute-start.9 = (bf16[112,1536]{1,0:T(8,128)(2,1)S(1)}, bf16[112,1536]{1,0:T(8,128)(2,1)S(1)}, u32[]{:S(2)}, u32[]{:S(2)}) collective-permute-start(bf16[112,1536]{1,0:T(8,128)(2,1)S(1)} %pad_maximum_fusion.6), channel_id=1, source_target_pairs={{0,4},{1,5},{2,6},{3,7},{4,0},{5,1},{6,2},{7,3},{8,12},{9,13},{10,... | collective-permute-start | bytes 1032200 | tf_op jit(solution)/shard_map/ppermute | solution.py:684
  293.2 59.1 %collective-permute-start.16 = (bf16[96,1536]{1,0:T(8,128)(2,1)S(1)}, bf16[96,1536]{1,0:T(8,128)(2,1)S(1)}, u32[]{:S(2)}, u32[]{:S(2)}) collective-permute-start(bf16[96,1536]{1,0:T(8,128)(2,1)S(1)} %fusion.22), channel_id=1, source_target_pairs={{0,16},{8,24},{16,0},{24,8},{1,17},{9,25},{17,1},{25,9},{2,18},{10... | collective-permute-start | bytes 884744 | tf_op jit(solution)/shard_map/ppermute | solution.py:684
  322.5 26.8 %collective-permute-start.21 = (bf16[96,3072]{1,0:T(8,128)(2,1)S(1)}, bf16[96,3072]{1,0:T(8,128)(2,1)S(1)}, u32[]{:S(2)}, u32[]{:S(2)}) collective-permute-start(bf16[96,3072]{1,0:T(8,128)(2,1)S(1)} %fusion.7), channel_id=1, source_target_pairs={{0,4},{1,5},{2,6},{3,7},{4,0},{5,1},{6,2},{7,3},{8,12},{9,13},{10,... | collective-permute-start | bytes 1769480 | tf_op jit(solution)/shard_map/ppermute | solution.py:684
  325.7 30.3 %collective-permute-start.10 = (bf16[112,1536]{1,0:T(8,128)(2,1)S(1)}, bf16[112,1536]{1,0:T(8,128)(2,1)S(1)}, u32[]{:S(2)}, u32[]{:S(2)}) collective-permute-start(bf16[112,1536]{1,0:T(8,128)(2,1)S(1)} %pad_maximum_fusion.7), channel_id=1, source_target_pairs={{0,16},{8,24},{16,0},{24,8},{1,17},{9,25},{17,1},{25,9},{2,18},{10... | collective-permute-start | bytes 1032200 | tf_op jit(solution)/shard_map/ppermute | solution.py:684
  351.0 11.6 %collective-permute-start.22 = (bf16[96,3072]{1,0:T(8,128)(2,1)S(1)}, bf16[96,3072]{1,0:T(8,128)(2,1)S(1)}, u32[]{:S(2)}, u32[]{:S(2)}) collective-permute-start(bf16[96,3072]{1,0:T(8,128)(2,1)S(1)} %fusion.11), channel_id=1, source_target_pairs={{0,16},{8,24},{16,0},{24,8},{1,17},{9,25},{17,1},{25,9},{2,18},{10... | collective-permute-start | bytes 1769480 | tf_op jit(solution)/shard_map/ppermute | solution.py:684
  352.4 16.0 %collective-permute-start.17 = (bf16[96,1536]{1,0:T(8,128)(2,1)S(1)}, bf16[96,1536]{1,0:T(8,128)(2,1)S(1)}, u32[]{:S(2)}, u32[]{:S(2)}) collective-permute-start(bf16[96,1536]{1,0:T(8,128)(2,1)S(1)} %add_convert_fusion.2.own_ref), channel_id=1, source_target_pairs={{0,8},{8,0},{16,24},{24,16},{1,9},{9,1},{17,25},{25,17},{2,10},{10... | collective-permute-start | bytes 884744 | tf_op jit(solution)/shard_map/ppermute | solution.py:684
  356.1 13.9 %collective-permute-start.11 = (bf16[96,1536]{1,0:T(8,128)(2,1)S(1)}, bf16[96,1536]{1,0:T(8,128)(2,1)S(1)}, u32[]{:S(2)}, u32[]{:S(2)}) collective-permute-start(bf16[96,1536]{1,0:T(8,128)(2,1)S(1)} %add_convert_fusion.3.own_ref), channel_id=1, source_target_pairs={{0,8},{8,0},{16,24},{24,16},{1,9},{9,1},{17,25},{25,17},{2,10},{10... | collective-permute-start | bytes 884744 | tf_op jit(solution)/shard_map/ppermute | solution.py:684
  362.7 8.9 %collective-permute-start.23 = (bf16[96,3072]{1,0:T(8,128)(2,1)S(1)}, bf16[96,3072]{1,0:T(8,128)(2,1)S(1)}, u32[]{:S(2)}, u32[]{:S(2)}) collective-permute-start(bf16[96,3072]{1,0:T(8,128)(2,1)S(1)} %add_convert_fusion.own_ref), channel_id=1, source_target_pairs={{0,8},{8,0},{16,24},{24,16},{1,9},{9,1},{17,25},{25,17},{2,10},{10... | collective-permute-start | bytes 1769480 | tf_op jit(solution)/shard_map/ppermute | solution.py:684
  (7 other events, 47.8 us)
